TPU v7x, 128 devices: a whole 4x4x4 slice. The times are simulated.
128 devices in a mesh: prow: 8 (over y, x_hi), pcol: 16 (over z, x_lo, core).
Axes of the slice: x: 4 (x_hi: 2, x_lo: 2; x = x_hi * 2 + x_lo), y: 4, z: 4, core: 2. Of those that a mesh axis runs over, the one named last changes fastest.
Arguments:
- root_sigma: float32 [12288, 12288], P('prow', 'pcol')
- pivot_diag: float32 [128, 2, 3072], P(None, None, 'prow'), may hold values from -6 to 6
- update_l: float32 [3072, 12288], P('prow', 'pcol'), may hold values from -0.078125 to 0.078125
- update_map: int32 [2, 48], replicated, may hold values from 0 to 95, as said below
Outputs:
- pivot_update: float32 [3072, 12288], P('prow', 'pcol')
- marginal_cov: float32 [128, 2, 3072], P(None, None, 'prow')
Inputs may be any that keep to these rules, and one draw needn't show every extreme that they name: `update_map`: for every child c and block i < 8, the entries r from i * 6 to (i + 1) * 6 - 1 are distinct, increasing, and all equal to i modulo 8.
All inputs are finite; a program needn't handle non-finite values.
Results may differ from a plain program's by a relative error of at most 0.0001.
Values sent between devices are 32-bit elements; how exact they have to be, the bound alone decides.
A program may use at most 128 MiB of HBM per device.

v0:
```python
import jax
import jax.numpy as jnp
from jax import lax
from jax.sharding import PartitionSpec as P

exact_mode = lax.Precision.HIGHEST


def swapped(block, axis, bit):
    count = lax.axis_size(axis)
    route = []
    for low in range(count):
        high = low | 1 << bit
        if high != low and high < count:
            route += [(low, high), (high, low)]
    return lax.ppermute(block, axis, route)


def pick_rows(stored, tile_ids, groups, tile_width):
    tile_count = stored.shape[0] // tile_width
    shaped = stored.reshape(tile_count, tile_width, stored.shape[1])
    chosen = jnp.take(shaped, tile_ids // groups, axis=0)
    return chosen.reshape(tile_ids.shape[0] * tile_width, stored.shape[1])


def local(root_sigma, pivot_diag, update_l, update_map):
    rows_grid = lax.axis_size("prow")
    cols_grid = lax.axis_size("pcol")
    half_grid = cols_grid // 2
    my_row = lax.axis_index("prow")
    my_col = lax.axis_index("pcol")
    my_child = my_col // half_grid
    col_block = my_col % half_grid
    tile_width = pivot_diag.shape[0]
    per_block = update_map.shape[1] // rows_grid
    own_map = jnp.take(update_map, my_child, axis=0)
    far_map = jnp.take(update_map, 1 - my_child, axis=0)
    own_rows = lax.dynamic_slice_in_dim(own_map, my_row * per_block, per_block)
    far_rows = lax.dynamic_slice_in_dim(far_map, my_row * per_block, per_block)
    own_select = pick_rows(root_sigma, own_rows, rows_grid, tile_width)
    far_select = pick_rows(root_sigma, far_rows, rows_grid, tile_width)
    partner = swapped(far_select, "pcol", half_grid.bit_length() - 1)
    row_count = own_select.shape[0]
    local_cols = root_sigma.shape[1] // tile_width
    col_ids = lax.dynamic_slice_in_dim(own_map, col_block * per_block, per_block)
    from_partner = (col_ids % cols_grid != my_col).astype(jnp.int32)
    position = col_ids // cols_grid + local_cols * from_partner
    joined = jnp.concatenate([own_select, partner], axis=1).reshape(
        row_count, 2 * local_cols, tile_width
    )
    update_block = jnp.take(joined, position, axis=1).reshape(row_count, per_block * tile_width)
    upd_dev = update_l.shape[1]
    piv_dev = update_l.shape[0]
    row_panel = update_l
    for level in range(half_grid.bit_length() - 1):
        received = swapped(row_panel, "pcol", level)
        upper_bit = my_col // 2**level % 2
        row_panel = jnp.where(
            upper_bit == 1,
            jnp.concatenate([received, row_panel], axis=1),
            jnp.concatenate([row_panel, received], axis=1),
        )
    initial = jnp.zeros((piv_dev, update_block.shape[1]), jnp.float32)
    pivot_update = initial - jnp.dot(
        row_panel,
        lax.all_gather(update_block, "prow", axis=0, tiled=True),
        precision=exact_mode,
        preferred_element_type=jnp.float32,
    )
    tiles_here = piv_dev // tile_width
    left_tiles = pivot_update.reshape(tiles_here, tile_width, upd_dev)
    right_tiles = update_l.reshape(tiles_here, tile_width, upd_dev)
    partial_diag = jnp.einsum(
        "qrk,qsk->rqs", left_tiles, right_tiles, precision=exact_mode
    ).reshape(tile_width, tiles_here * tile_width)
    first_slot = partial_diag * (my_child == 0).astype(jnp.float32)
    second_slot = partial_diag * (my_child == 1).astype(jnp.float32)
    stacked = jnp.stack([first_slot, second_slot], axis=1)
    summed = lax.psum(stacked, "pcol")
    marginal_cov = pivot_diag - summed
    return (pivot_update, marginal_cov)


def solution(mesh):
    placed = (P("prow", "pcol"), P(None, None, "prow"), P("prow", "pcol"), P())
    return jax.shard_map(
        local,
        mesh=mesh,
        in_specs=placed,
        out_specs=(P("prow", "pcol"), P(None, None, "prow")),
        check_vma=False,
    )
```

profile of v0, /device:TPU:1, one launch (start us, length us, event | category | flops | bytes accessed | tf_op | source)
XLA Modules:
  0.0 471.7 jit_solution(18198196913811666383)
XLA Ops:
  8.1 3.0 gather_fusion.2
  11.2 1.7 broadcast_select_fusion
  12.9 4.4 collective-permute-start.3
  17.3 3.0 gather_fusion.1
  20.4 1.7 broadcast_select_fusion.1
  22.1 2.5 concatenate.32
  24.6 1.9 copy.14
  26.6 42.1 %collective-permute-done.3 = f32[768,768]{1,0:T(8,128)} collective-permute-done((f32[768,768]{1,0:T(8,128)}, f32[768,768]{1,0:T(8,128)}, u32[]{:S(2)}, u32[]{:S(2)}) %collective-permute-start.3) | collective-permute-done | bytes 2359328 | tf_op jit(solution)/shard_map/ppermute | solution.py:16
  68.6 2.0 copy.13
  70.6 2.0 copy.15
  72.7 4.8 %pad_maximum_fusion = f32[768,12,128]{2,0,1:T(8,128)} fusion(f32[768,6,128]{2,0,1:T(8,128)} %copy.15, f32[768,6,128]{2,0,1:T(8,128)} %copy.14), kind=kLoop, calls=%fused_computation.11 | loop fusion | flops 1179648 | bytes 9437184 | tf_op jit(solution)/shard_map/concatenate | solution.py:48
  77.5 3.0 gather_fusion
  80.5 2.0 copy.16
  82.5 3.4 bitcast_select_fusion
  88.4 2.6 collective-permute-done
  91.0 2.0 maximum_select_fusion.3
  93.0 1.3 collective-permute-start.1
  94.3 76.6 %collective-permute-done.1 = f32[384,1536]{1,0:T(8,128)} collective-permute-done((f32[384,1536]{1,0:T(8,128)S(1)}, f32[384,1536]{1,0:T(8,128)}, u32[]{:S(2)}, u32[]{:S(2)}) %collective-permute-start.1) | collective-permute-done | bytes 2359328 | tf_op jit(solution)/shard_map/ppermute | solution.py:16
  171.0 5.4 %maximum_select_fusion.2 = f32[384,3072]{1,0:T(8,128)} fusion(f32[384,1536]{1,0:T(8,128)S(1)} %maximum_select_fusion.3, f32[384,1536]{1,0:T(8,128)} %collective-permute-done.1, pred[]{:T(512)S(6)} %eq.23), kind=kLoop, calls=%fused_computation.10 | loop fusion | flops 3538944 | bytes 9437185 | tf_op jit(solution)/shard_map/jit(_where)/select_n | solution.py:58
  177.3 101.4 %collective-permute-done.2 = f32[384,3072]{1,0:T(8,128)} collective-permute-done((f32[384,3072]{1,0:T(8,128)}, f32[384,3072]{1,0:T(8,128)}, u32[]{:S(2)}, u32[]{:S(2)}) %collective-permute-start.2) | collective-permute-done | bytes 4718624 | tf_op jit(solution)/shard_map/ppermute | solution.py:16
  278.7 36.5 %all-gather.2.cloned.1.call-done = f32[6144,768]{0,1:T(8,128)} async-done(((f32[768,768]{0,1:T(8,128)}), f32[6144,768]{0,1:T(8,128)}) %all-gather.2.cloned.1.call-update) | async-done | bytes 18874384 | tf_op jit(solution)/shard_map/all_gather | solution.py:66
  315.2 29.2 %fusion.7 = f32[384,768]{1,0:T(8,128)S(1)} fusion(f32[6144,768]{0,1:T(8,128)} %all-gather.2.cloned.1.call-done, f32[384,3072]{1,0:T(8,128)} %maximum_select_fusion.2, f32[384,3072]{1,0:T(8,128)} %collective-permute-done.2, pred[]{:T(512)S(6)} %eq.22), kind=kOutput, calls=%fused_computation.15 | convolution fusion | flops 21750644736 | bytes 29491200 | tf_op jit(solution)/shard_map/dot_general | solution.py:64
  347.1 115.8 %all-reduce.2.cloned.1.call-done = f32[128,2,384]{2,1,0:T(2,128)} async-done(((f32[128,2,384]{2,1,0:T(2,128)}), f32[128,2,384]{2,1,0:T(2,128)}) %all-reduce.2.cloned.1.call-update) | async-done | bytes 393232 | tf_op jit(solution)/shard_map/psum | solution.py:79
  462.9 1.9 sub.38
  (22 shorter events, 7.2 us)
Async XLA Ops:
  7.2 308.0 %all-gather.2.cloned.1.call-start = ((), (), s32[]{:S(2)}) async-start(), calls=%async_computation | async-start | bytes 21233664 | tf_op jit(solution)/shard_map/all_gather | solution.py:66
  12.9 55.7 %collective-permute-start.3 = (f32[768,768]{1,0:T(8,128)}, f32[768,768]{1,0:T(8,128)}, u32[]{:S(2)}, u32[]{:S(2)}) collective-permute-start(f32[768,768]{1,0:T(8,128)} %bitcast.4), channel_id=1, source_target_pairs={{0,8},{8,0},{1,9},{9,1},{2,10},{10,2},{3,11},{11,3},{4,12},{12,4},... | collective-permute-start | bytes 7077896 | tf_op jit(solution)/shard_map/ppermute | solution.py:16
  85.9 1.3 copy-start
  85.9 377.0 %all-reduce.2.cloned.1.call-start = ((), (), s32[]{:S(2)}) async-start(), calls=%async_computation.1 | async-start | bytes 786432 | tf_op jit(solution)/shard_map/psum | solution.py:79
  87.2 3.8 collective-permute-start
  93.0 77.9 %collective-permute-start.1 = (f32[384,1536]{1,0:T(8,128)S(1)}, f32[384,1536]{1,0:T(8,128)}, u32[]{:S(2)}, u32[]{:S(2)}) collective-permute-start(f32[384,1536]{1,0:T(8,128)S(1)} %maximum_select_fusion.3), channel_id=1, source_target_pairs={{0,2},{2,0},{1,3},{3,1},{4,6},{6,4},{5,7},{7,5},{8,10},{10,8},{9,1... | collective-permute-start | bytes 7077896 | tf_op jit(solution)/shard_map/ppermute | solution.py:16
  176.3 102.4 %collective-permute-start.2 = (f32[384,3072]{1,0:T(8,128)}, f32[384,3072]{1,0:T(8,128)}, u32[]{:S(2)}, u32[]{:S(2)}) collective-permute-start(f32[384,3072]{1,0:T(8,128)} %maximum_select_fusion.2), channel_id=1, source_target_pairs={{0,4},{4,0},{1,5},{5,1},{2,6},{6,2},{3,7},{7,3},{8,12},{12,8},{9,1... | collective-permute-start | bytes 14155784 | tf_op jit(solution)/shard_map/ppermute | solution.py:16
  344.4 2.8 copy-start.1
  344.4 118.5 %copy-start.2 = (f32[128,2,384]{2,1,0:T(2,128)S(1)}, f32[128,2,384]{2,1,0:T(2,128)}, u32[]{:S(2)}) copy-start(f32[128,2,384]{2,1,0:T(2,128)} %param.9) | copy-start | bytes 1179652
Sparse Core Ops, SparseCore 0:
  86.1 229.0 all-gather.1
  347.2 115.6 all-reduce.1
where the time goes:
time: 472 us
  waiting for transfers between devices  375 us (79%)
  matrix products  30.4 us (6%)
  other arithmetic  23 us (5%)
  local copies, waits for them, and re-layouts  21.1 us (4%)
  between operations  14.2 us (3%)
  starting transfers between devices  8.03 us (2%)
    ppermute x4, waiting for transfers between devices, swapped(): return lax.ppermute(block, axis, route)  223 us
    psum x1, waiting for transfers between devices, local(): summed = lax.psum(stacked, 'pcol')  116 us
    all_gather x1, waiting for transfers between devices, local(): lax.all_gather(update_block, 'prow', axis=0, tiled=True)  36.5 us
    dot_general x1, matrix products, local(): jnp.dot(row_panel, lax.all_gather(update_block, 'prow', axis=0, tiled=Tru...  29.2 us
  transfers between devices with their start and end apart: 6, of which 6 were waited for; matrix products, arithmetic and copies ran while one was open for 4% of the time, Pallas kernels for 0%

commit v1 on v0

v1 whole, which is shorter than its diff:
```python
import jax
import jax.numpy as jnp
from jax import lax
from jax.experimental import pallas as pl
from jax.experimental.pallas import tpu as pltpu
from jax.sharding import PartitionSpec as P

MESH = pl.DeviceIdType.MESH
F32, BF16 = jnp.float32, jnp.bfloat16
NT = (((1,), (1,)), ((), ()))


def split(x):
    hi = x.astype(BF16)
    return hi, (x - hi.astype(F32)).astype(BF16)


def kernel(umap, sig, pd, l_ref, c_out, m_out, fs, rc, stf, bhi, blo, lb, ahi, alo, prod, xr, zr, tr, dsend, dr, g,
           zs_s, zs_r, cs_s, cs_r, ls_s, l_r, fw_s, x_s, x_r, z_s, z_r, t_s, t_r, d_s, d_r, g_s, g_r):
    me_r, me_c = lax.axis_index("prow"), lax.axis_index("pcol")
    y, xh = me_r // 2, me_r % 2
    half, j = me_c // 8, me_c % 8
    zl, xl, k = j // 4, (j // 2) % 2, j % 2
    chunks = fs.shape[0]
    width = fs.shape[1]
    tile = sig.shape[1]
    tiles = 2 * chunks

    def dev(y_, xh_, zl_, xl_, k_):
        return (y_ * 2 + xh_, half * 8 + zl_ * 4 + xl_ * 2 + k_)

    partner = (me_r, (me_c + 8) % 16)
    other_core = dev(y, xh, zl, xl, 1 - k)
    x_peer = dev(y, xh, zl, 1 - xl, k)
    z_peer = dev(y, xh, 1 - zl, xl, k)
    y_final = 2 * zl + 1 - xl
    deliver = (y_final * 2 + (xh + k) % 2, half * 8 + me_r)
    source = ((2 * zl + xl) * 2 + k, half * 8 + (y // 2) * 4 + (1 - y % 2) * 2 + (xh + k) % 2)

    def copy(src, dst, ssem, rsem, to):
        return pltpu.make_async_remote_copy(
            src_ref=src, dst_ref=dst, send_sem=ssem, recv_sem=rsem, device_id=to, device_id_type=MESH)

    barrier = pltpu.get_barrier_semaphore()

    def greet(to):
        pl.semaphore_signal(barrier, inc=1, device_id=to, device_id_type=MESH)

    for d in range(1, 16):
        greet((me_r, (me_c + d) % 16))
    for d in range(1, 4):
        for kk in range(2):
            greet(dev((y + d) % 4, xh, zl, xl, kk))
    for kk in range(2):
        greet(dev(y, 1 - xh, zl, xl, kk))
    greet(source)
    pl.semaphore_wait(barrier, 24)

    def far_copy(q):
        return copy(fs.at[q], rc.at[q], zs_s.at[q], zs_r.at[q], partner)

    for q in range(chunks):
        for h in range(2):
            row = umap[1 - half, me_r * tiles + 2 * q + h] // 8
            fs[q, h * tile:(h + 1) * tile, :] = sig[row]
        far_copy(q).start()

    own_l = [copy(l_ref, lb.at[y, k], ls_s.at[d - 1], l_r.at[y, k], dev((y + d) % 4, xh, zl, xl, 0)) for d in range(1, 4)]
    own_l.append(copy(l_ref, lb.at[y, k], ls_s.at[3], l_r.at[y, k], dev(y, 1 - xh, zl, xl, 1)))
    own_l[3].start()
    for c in own_l[:3]:
        c.start()
    near_l = copy(l_ref, lb.at[y, k], ls_s.at[4], l_r.at[y, k], other_core)
    stay_l = pltpu.make_async_copy(l_ref, lb.at[y, 0], l_r.at[y, 0])

    @pl.when(k == 1)
    def _():
        near_l.start()

    @pl.when(k == 0)
    def _():
        stay_l.start()

    def forward(kk, d):
        return copy(lb.at[y, kk], lb.at[y, kk], fw_s.at[kk, d - 1], l_r.at[y, kk], dev((y + d) % 4, xh, zl, xl, 1))

    def core_copy(q):
        return copy(stf.at[k, q], stf.at[k, q], cs_s.at[q], cs_r.at[q], other_core)

    def take_s(q):
        far_copy(q).wait_recv()
        for h in range(2):
            row = umap[half, me_r * tiles + 2 * q + h] // 8
            near = sig[row]
            far = rc[q, h * tile:(h + 1) * tile, :]
            for s in range(tiles):
                col = umap[half, j * tiles + s]
                spot = col // 16 + tiles * (((col // 8) % 2 + half) % 2)
                x = near[:, :tile]
                for c in range(1, 2 * tiles):
                    lanes = slice((c % tiles) * tile, (c % tiles + 1) * tile)
                    x = jnp.where(spot == c, (near if c < tiles else far)[:, lanes], x)
                stf[k, q, s * tile:(s + 1) * tile, h * tile:(h + 1) * tile] = x.T
        core_copy(q).start()
        hi, lo = split(stf[k, q])
        bhi[q, k] = hi
        blo[q, k] = lo
        copy(stf.at[1 - k, q], stf.at[1 - k, q], cs_s.at[q], cs_r.at[q], other_core).wait_recv()
        hi, lo = split(stf[1 - k, q])
        bhi[q, 1 - k] = hi
        blo[q, 1 - k] = lo

    def x_copy(b, q):
        return copy(prod.at[xl + 2 * b, q], xr.at[b, q], x_s.at[b, q], x_r.at[b, q], x_peer)

    def slot(t, carry):
        yp = (y + t + (t // 2) * (1 - 2 * (t % 2))) % 4
        for kk in range(2):
            copy(lb.at[yp, kk], lb.at[yp, kk], ls_s.at[0], l_r.at[yp, kk], other_core).wait_recv()

        @pl.when((t == 0) & (k == 1))
        def _():
            for d in (1, 3, 2):
                for kk in range(2):
                    forward(kk, d).start()

        for kk in range(2):
            hi, lo = split(lb[yp, kk])
            ahi[kk] = hi
            alo[kk] = lo
        for q in range(chunks):
            @pl.when(t == 0)
            def _():
                take_s(q)

            total = jnp.zeros((ahi.shape[1], width), F32)
            for kk in range(2):
                total += jnp.dot(ahi[kk], bhi[q, kk], preferred_element_type=F32)
                total += jnp.dot(ahi[kk], blo[q, kk], preferred_element_type=F32)
                total += jnp.dot(alo[kk], bhi[q, kk], preferred_element_type=F32)
            prod[yp, q] = total

            @pl.when(yp % 2 == xl)
            def _():
                x_copy(yp // 2, q).start()
        return carry

    lax.fori_loop(0, 4, slot, 0)

    y_sent = 2 * (1 - zl) + 1 - xl

    def z_copy(q):
        return copy(prod.at[y_sent, q], zr.at[q], z_s.at[q], z_r.at[q], z_peer)

    def t_copy(q):
        return copy(prod.at[y_final, q], tr.at[q], t_s.at[q], t_r.at[q], deliver)

    for q in range(chunks):
        x_copy(1 - zl, q).wait_recv()
        prod[y_sent, q] = prod[y_sent, q] + xr[1 - zl, q]
        z_copy(q).start()
    for q in range(chunks):
        x_copy(zl, q).wait_recv()
        z_copy(q).wait_recv()
        prod[y_final, q] = -(prod[y_final, q] + xr[zl, q] + zr[q])
        t_copy(q).start()

    diag = [jnp.zeros((tile, tile), F32) for _ in range(l_ref.shape[0] // tile)]
    for q in range(chunks):
        t_copy(q).wait_recv()
        cols = slice(q * width, (q + 1) * width)
        c_out[:, cols] = tr[q]
        for t in range(len(diag)):
            rows = slice(t * tile, (t + 1) * tile)
            diag[t] += lax.dot_general(tr[q, rows], l_ref[rows, cols], NT, precision=lax.Precision.HIGHEST,
                                       preferred_element_type=F32)
    for t in range(len(diag)):
        dsend[:, :, t * tile:(t + 1) * tile] = diag[t].reshape(8, tile // 8, tile)

    def d_copy(d):
        to = (j + d) % 8
        return copy(dsend.at[to], dr.at[j], d_s.at[d], d_r.at[j], (me_r, half * 8 + to))

    def d_from(d):
        frm = (j + d) % 8
        return copy(dsend.at[frm], dr.at[frm], d_s.at[d], d_r.at[frm], (me_r, half * 8 + frm))

    for d in range(1, 8):
        d_copy(d).start()
    dr[j] = dsend[j]
    for d in range(1, 8):
        d_from(d).wait_recv()
    total = dr[0]
    for d in range(1, 8):
        total += dr[d]
    g[me_c] = total

    def g_copy(d):
        return copy(g.at[me_c], g.at[me_c], g_s.at[d], g_r.at[me_c], (me_r, (me_c + d) % 16))

    def g_from(d):
        frm = (me_c + d) % 16
        return copy(g.at[frm], g.at[frm], g_s.at[d], g_r.at[frm], (me_r, frm))

    for d in range(1, 16):
        g_copy(d).start()
    for d in range(1, 16):
        g_from(d).wait_recv()
    for h in range(2):
        m_out[:, h, :] = pd[:, h, :] - g[h * 8:(h + 1) * 8].reshape(tile, -1)

    for q in range(chunks):
        far_copy(q).wait_send()
        core_copy(q).wait_send()
        z_copy(q).wait_send()
        t_copy(q).wait_send()
        for b in range(2):
            x_copy(b, q).wait_send()
    for c in own_l:
        c.wait_send()

    @pl.when(k == 1)
    def _():
        near_l.wait_send()
        for d in range(1, 4):
            for kk in range(2):
                forward(kk, d).wait_send()

    for d in range(1, 8):
        d_copy(d).wait_send()
    for d in range(1, 16):
        g_copy(d).wait_send()


def local(root_sigma, pivot_diag, update_l, update_map):
    tile = pivot_diag.shape[0]
    rows, cols = update_l.shape
    chunks = 3
    width = cols // chunks
    sem = pltpu.SemaphoreType.DMA
    vmem = pl.BlockSpec(memory_space=pltpu.VMEM)
    return pl.pallas_call(
        kernel,
        out_shape=(jax.ShapeDtypeStruct(update_l.shape, F32), jax.ShapeDtypeStruct(pivot_diag.shape, F32)),
        in_specs=[pl.BlockSpec(memory_space=pltpu.SMEM), vmem, vmem, vmem],
        out_specs=(vmem, vmem),
        scratch_shapes=[
            pltpu.VMEM((chunks, width, cols), F32),
            pltpu.VMEM((chunks, width, cols), F32),
            pltpu.VMEM((2, chunks, cols, width), F32),
            pltpu.VMEM((chunks, 2, cols, width), BF16),
            pltpu.VMEM((chunks, 2, cols, width), BF16),
            pltpu.VMEM((4, 2, rows, cols), F32),
            pltpu.VMEM((2, rows, cols), BF16),
            pltpu.VMEM((2, rows, cols), BF16),
            pltpu.VMEM((4, chunks, rows, width), F32),
            pltpu.VMEM((2, chunks, rows, width), F32),
            pltpu.VMEM((chunks, rows, width), F32),
            pltpu.VMEM((chunks, rows, width), F32),
            pltpu.VMEM((8, tile // 8, rows), F32),
            pltpu.VMEM((8, tile // 8, rows), F32),
            pltpu.VMEM((16, tile // 8, rows), F32),
            sem((chunks,)), sem((chunks,)), sem((chunks,)), sem((chunks,)),
            sem((5,)), sem((4, 2)), sem((2, 3)),
            sem((2, chunks)), sem((2, chunks)), sem((chunks,)), sem((chunks,)), sem((chunks,)), sem((chunks,)),
            sem((8,)), sem((8,)), sem((16,)), sem((16,)),
        ],
        compiler_params=pltpu.CompilerParams(
            collective_id=0, has_side_effects=True, vmem_limit_bytes=60 * 2**20),
        name="selected_inverse",
    )(update_map, root_sigma.reshape(-1, tile, root_sigma.shape[1]), pivot_diag, update_l)


def solution(mesh):
    placed = (P("prow", "pcol"), P(None, None, "prow"), P("prow", "pcol"), P())
    return jax.shard_map(
        local,
        mesh=mesh,
        in_specs=placed,
        out_specs=(P("prow", "pcol"), P(None, None, "prow")),
        check_vma=False,
    )
```

time: 472 us -> 187 us (0.40)
  waiting for transfers between devices: 375 us -> 0 us
  Pallas kernels: 0 us -> 183 us
  matrix products: 30.4 us -> 0 us
  other arithmetic: 23 us -> 0 us
  local copies, waits for them, and re-layouts: 21.1 us -> 3.16 us
  between operations: 14.2 us -> 0.65 us
  starting transfers between devices: 8.03 us -> 0 us
    ppermute x4 -> x0, waiting for transfers between devices: 223 us -> none  [swapped(): return lax.ppermute(block, axis, route)]
    pallas_call x0 -> x1, Pallas kernels: none -> 183 us  [local(): pl.pallas_call(kernel, out_shape=(jax.ShapeDtypeStruct(update_l.shape, F3...]
    psum x1 -> x0, waiting for transfers between devices: 116 us -> none  [local(): summed = lax.psum(stacked, 'pcol')]
    all_gather x1 -> x0, waiting for transfers between devices: 36.5 us -> none  [local(): lax.all_gather(update_block, 'prow', axis=0, tiled=True)]
    dot_general x2 -> x0, matrix products: 30.4 us -> none  [the longest x1 29.2 us: local(): jnp.dot(row_panel, lax.all_gather(update_block, 'prow', axis=0, tiled=Tru...]
    select_n x6 -> x0, other arithmetic: 15 us -> none  [the longest x2 7.36 us: local(): jnp.where(upper_bit == 1, jnp.concatenate([received, row_panel], axis=1),...]
    gather x4 -> x0, local copies, waits for them, and re-layouts: 11.1 us -> none  [the longest x2 6.07 us: pick_rows(): chosen = jnp.take(shaped, tile_ids // groups, axis=0)]
    ppermute x4 -> x0, starting transfers between devices: 7.95 us -> none  [swapped(): return lax.ppermute(block, axis, route)]
  transfers between devices with their start and end apart: 6 -> 0, of which waited for: 6 -> 0; matrix products, arithmetic and copies ran while one was open for 4% -> 0% of each run, Pallas kernels for 0% -> 0%
where the time goes in v1:
time: 187 us
  Pallas kernels  183 us (98%)
  local copies, waits for them, and re-layouts  3.16 us (2%)
    pallas_call x1, Pallas kernels, local(): pl.pallas_call(kernel, out_shape=(jax.ShapeDtypeStruct(update_l.shape, F3...  183 us

profile of v1, /device:TPU:1, one launch (start us, length us, event | category | flops | bytes accessed | tf_op | source)
XLA Modules:
  0.0 187.1 jit_solution(16779170961109610016)
XLA Ops:
  0.6 183.3 %selected_inverse.1 = (f32[384,768]{1,0:T(8,128)}, f32[128,2,384]{2,1,0:T(2,128)}) custom-call(s32[2,48]{1,0:T(2,128)} %umap.1, f32[12,128,768]{2,1,0:T(8,128)} %bitcast.1, f32[128,2,384]{2,1,0:T(2,128)} %pd.1, f32[384,768]{1,0:T(8,128)} %l_ref.1), custom_call_target="tpu_custom_call" | custom-call | tf_op jit(solution)/shard_map/selected_inverse/pallas_call | solution.py:242
  183.9 0.0 copy-start
  184.0 2.4 %copy.8 = f32[384,768]{1,0:T(8,128)} copy(f32[384,768]{1,0:T(8,128)} %get-tuple-element.4) | data formatting | bytes 2359296
  186.4 0.0 copy-done
  186.4 0.7 copy.9
Async XLA Ops:
  183.9 2.4 %copy-start = (f32[128,2,384]{2,1,0:T(2,128)S(1)}, f32[128,2,384]{2,1,0:T(2,128)}, u32[]{:S(2)}) copy-start(f32[128,2,384]{2,1,0:T(2,128)} %get-tuple-element.5) | copy-start | bytes 1179652

commit v2 on v1

v2 whole, which is shorter than its diff:
```python
import jax
import jax.numpy as jnp
from jax import lax
from jax.experimental import pallas as pl
from jax.experimental.pallas import tpu as pltpu
from jax.sharding import PartitionSpec as P

MESH = pl.DeviceIdType.MESH
F32, BF16 = jnp.float32, jnp.bfloat16
NT = (((1,), (1,)), ((), ()))


def split(x):
    hi = x.astype(BF16)
    return hi, (x - hi.astype(F32)).astype(BF16)


def kernel(umap, sig, pd, l_ref, c_out, m_out, fs, rc, stf, bhi, blo, lx, lb, ahi, alo, prod, xr, zr, fin, leg, got, dsend, dr, g,
           zs_s, zs_r, cs_s, cs_r, lx_s, lx_r, l_s, f_s, l_r, x_s, x_r, z_s, z_r, a_s, a_r, b_s, b_r, d_s, d_r, g_s, g_r):
    me_r, me_c = lax.axis_index("prow"), lax.axis_index("pcol")
    y, xh = me_r // 2, me_r % 2
    half, j = me_c // 8, me_c % 8
    zl, xl, k = j // 4, (j // 2) % 2, j % 2
    chunks, width = fs.shape[0], fs.shape[1]
    tile = sig.shape[1]
    tiles = 2 * chunks
    rows = l_ref.shape[0]
    part = rows // 4
    steps = 4 * chunks

    def dev(y_, xh_, zl_, xl_, k_):
        return (y_ * 2 + xh_, half * 8 + zl_ * 4 + xl_ * 2 + k_)

    partner = (me_r, (me_c + 8) % 16)
    other_core = dev(y, xh, zl, xl, 1 - k)
    x_peer = dev(y, xh, zl, 1 - xl, k)
    z_peer = dev(y, xh, 1 - zl, xl, k)

    def copy(src, dst, ssem, rsem, to):
        return pltpu.make_async_remote_copy(
            src_ref=src, dst_ref=dst, send_sem=ssem, recv_sem=rsem, device_id=to, device_id_type=MESH)

    barrier = pltpu.get_barrier_semaphore()

    def greet(to):
        pl.semaphore_signal(barrier, inc=1, device_id=to, device_id_type=MESH)

    for d in range(1, 16):
        greet((me_r, (me_c + d) % 16))
    for d in range(4):
        greet(dev((y + d) % 4, 1 - xh, zl, xl, k))
        if d > 0:
            for kk in range(2):
                greet(dev((y + d) % 4, xh, zl, xl, kk))
    pl.semaphore_wait(barrier, 25)

    def cross():
        return copy(l_ref, lx, lx_s, lx_r, dev(y, 1 - xh, zl, xl, k))

    def spread(src, core, sems, d):
        return copy(src, lb.at[y, k], sems.at[d], l_r.at[y, k], dev((y + d) % 4, xh, zl, xl, core))

    def spread_start(src, core, sems):
        for d in (1, 3, 2):
            spread(src, core, sems, d).start()

        @pl.when(k != core)
        def _():
            spread(src, core, sems, 0).start()

        @pl.when(k == core)
        def _():
            pltpu.make_async_copy(src, lb.at[y, core], l_r.at[y, core]).start()

    def spread_end(src, core, sems):
        for d in (1, 3, 2):
            spread(src, core, sems, d).wait_send()

        @pl.when(k != core)
        def _():
            spread(src, core, sems, 0).wait_send()

    cross().start()

    def far_copy(q):
        return copy(fs.at[q], rc.at[q], zs_s.at[q], zs_r.at[q], partner)

    for q in range(chunks):
        for h in range(2):
            row = umap[1 - half, me_r * tiles + 2 * q + h] // 8
            fs[q, h * tile:(h + 1) * tile, :] = sig[row]
        far_copy(q).start()

    spread_start(l_ref, 0, l_s)

    def core_copy(kk, q):
        return copy(stf.at[kk, q], stf.at[kk, q], cs_s.at[q], cs_r.at[q], other_core)

    def take_s(q):
        far_copy(q).wait_recv()
        for h in range(2):
            row = umap[half, me_r * tiles + 2 * q + h] // 8
            near = sig[row]
            far = rc[q, h * tile:(h + 1) * tile, :]
            for s in range(tiles):
                col = umap[half, j * tiles + s]
                spot = col // 16 + tiles * (((col // 8) % 2 + half) % 2)
                x = near[:, :tile]
                for c in range(1, 2 * tiles):
                    lanes = slice((c % tiles) * tile, (c % tiles + 1) * tile)
                    x = jnp.where(spot == c, (near if c < tiles else far)[:, lanes], x)
                stf[k, q, s * tile:(s + 1) * tile, h * tile:(h + 1) * tile] = x.T
        core_copy(k, q).start()
        hi, lo = split(stf[k, q])
        bhi[q, k] = hi
        blo[q, k] = lo
        core_copy(1 - k, q).wait_recv()
        hi, lo = split(stf[1 - k, q])
        bhi[q, 1 - k] = hi
        blo[q, 1 - k] = lo

    def where_of(n):
        last = n // (3 * chunks)
        t = (1 - k) * ((1 - last) * (n % 3) + last * 3) + k * (n // chunks)
        q = (1 - k) * ((1 - last) * (n // 3) + last * (n - 3 * chunks)) + k * (n % chunks)
        return t, q, t + (t // 2) * (1 - 2 * (t % 2))

    def x_copy(t, q):
        return copy(prod.at[t, q, pl.ds(2 * part * (1 - xl), 2 * part)], xr.at[t, q], x_s.at[t, q], x_r.at[t, q], x_peer)

    def z_copy(t, q):
        return copy(xr.at[t, q, pl.ds(part * (1 - zl), part)], zr.at[t, q], z_s.at[t, q], z_r.at[t, q], z_peer)

    def a_copy(t, q, dy):
        return copy(fin.at[t, q], leg.at[y, q], a_s.at[t, q], a_r.at[y, q], dev((y + dy) % 4, (xh + k) % 2, zl, xl, k))

    spot_b = pl.ds(2 * part * xl + part * zl, part)

    def b_copy(ys, q):
        return copy(leg.at[ys, q], got.at[q, spot_b], b_s.at[ys, q], b_r.at[q, xl, zl], dev(y, xh, ys // 2, ys % 2, (xh + k) % 2))

    def b_stays(ys):
        return (ys == 2 * zl + xl) & (xh == 0)

    lag_x, lag_z, lag_a = 2, 4, 6

    def step(n, carry):
        @pl.when(n < steps)
        def _():
            t, q, dy = where_of(n)
            yp = (y + dy) % 4

            @pl.when(t == 0)
            def _():
                take_s(q)

            @pl.when(n == 1 - k)
            def _():
                cross().wait_recv()
                spread_start(lx, 1, f_s)

            @pl.when(q == 0)
            def _():
                for kk in range(2):
                    copy(lb.at[yp, kk], lb.at[yp, kk], l_s.at[0], l_r.at[yp, kk], other_core).wait_recv()
                    hi, lo = split(lb[yp, kk])
                    ahi[t, kk] = hi
                    alo[t, kk] = lo

            total = jnp.zeros((rows, width), F32)
            for kk in range(2):
                total += jnp.dot(ahi[t, kk], bhi[q, kk], preferred_element_type=F32)
                total += jnp.dot(ahi[t, kk], blo[q, kk], preferred_element_type=F32)
                total += jnp.dot(alo[t, kk], bhi[q, kk], preferred_element_type=F32)
            prod[t, q] = total
            x_copy(t, q).start()

        @pl.when((n >= lag_x) & (n < steps + lag_x))
        def _():
            t, q, _ = where_of(n - lag_x)
            x_copy(t, q).wait_recv()
            xr[t, q] = xr[t, q] + prod[t, q, pl.ds(2 * part * xl, 2 * part)]
            z_copy(t, q).start()

        @pl.when((n >= lag_z) & (n < steps + lag_z))
        def _():
            t, q, dy = where_of(n - lag_z)
            z_copy(t, q).wait_recv()
            done = -(xr[t, q, pl.ds(part * zl, part)] + zr[t, q])
            here = (t == 0) & (k == 0)

            @pl.when(here)
            def _():
                leg[y, q] = done

            @pl.when(jnp.logical_not(here))
            def _():
                fin[t, q] = done
                a_copy(t, q, dy).start()

        @pl.when(n >= lag_a)
        def _():
            t, q, dy = where_of(n - lag_a)
            ys = (y + 4 - dy) % 4

            @pl.when((t > 0) | (k > 0))
            def _():
                copy(leg.at[ys, q], leg.at[ys, q], a_s.at[0, 0], a_r.at[ys, q], other_core).wait_recv()

            @pl.when(b_stays(ys))
            def _():
                got[q, spot_b] = leg[ys, q]

            @pl.when(jnp.logical_not(b_stays(ys)))
            def _():
                b_copy(ys, q).start()
        return carry

    lax.fori_loop(0, steps + lag_a, step, 0)

    diag = [jnp.zeros((tile, tile), F32) for _ in range(rows // tile)]
    for q in range(chunks):
        for xs in range(2):
            for zs in range(2):
                here = (zs == zl) & (xs == xl) & (xh == 0)

                @pl.when(jnp.logical_not(here))
                def _():
                    spot = got.at[q, pl.ds(2 * part * xs + part * zs, part)]
                    copy(spot, spot, b_s.at[0, 0], b_r.at[q, xs, zs], other_core).wait_recv()
        cols = slice(q * width, (q + 1) * width)
        c_out[:, cols] = got[q]
        for t in range(len(diag)):
            span = slice(t * tile, (t + 1) * tile)
            diag[t] += lax.dot_general(got[q, span], l_ref[span, cols], NT, precision=lax.Precision.HIGHEST,
                                       preferred_element_type=F32)
    for t in range(len(diag)):
        dsend[:, :, t * tile:(t + 1) * tile] = diag[t].reshape(8, tile // 8, tile)

    def d_copy(d):
        to = (j + d) % 8
        return copy(dsend.at[to], dr.at[j], d_s.at[d], d_r.at[j], (me_r, half * 8 + to))

    def d_from(d):
        frm = (j + d) % 8
        return copy(dsend.at[frm], dr.at[frm], d_s.at[d], d_r.at[frm], (me_r, half * 8 + frm))

    for d in range(1, 8):
        d_copy(d).start()
    dr[j] = dsend[j]
    for d in range(1, 8):
        d_from(d).wait_recv()
    total = dr[0]
    for d in range(1, 8):
        total += dr[d]
    g[me_c] = total

    def g_copy(d):
        return copy(g.at[me_c], g.at[me_c], g_s.at[d], g_r.at[me_c], (me_r, (me_c + d) % 16))

    def g_from(d):
        frm = (me_c + d) % 16
        return copy(g.at[frm], g.at[frm], g_s.at[d], g_r.at[frm], (me_r, frm))

    for d in range(1, 16):
        g_copy(d).start()
    for d in range(1, 16):
        g_from(d).wait_recv()
    for h in range(2):
        m_out[:, h, :] = pd[:, h, :] - g[h * 8:(h + 1) * 8].reshape(tile, -1)

    cross().wait_send()
    spread_end(l_ref, 0, l_s)
    spread_end(lx, 1, f_s)
    for q in range(chunks):
        far_copy(q).wait_send()
        core_copy(k, q).wait_send()

    def sent(n, carry):
        t, q, dy = where_of(n)
        ys = (y + 4 - dy) % 4
        x_copy(t, q).wait_send()
        z_copy(t, q).wait_send()

        @pl.when((t > 0) | (k > 0))
        def _():
            a_copy(t, q, dy).wait_send()

        @pl.when(jnp.logical_not(b_stays(ys)))
        def _():
            b_copy(ys, q).wait_send()
        return carry

    lax.fori_loop(0, steps, sent, 0)
    for d in range(1, 8):
        d_copy(d).wait_send()
    for d in range(1, 16):
        g_copy(d).wait_send()


def local(root_sigma, pivot_diag, update_l, update_map):
    tile = pivot_diag.shape[0]
    rows, cols = update_l.shape
    chunks = 3
    width = cols // chunks
    sem = pltpu.SemaphoreType.DMA
    vmem = pl.BlockSpec(memory_space=pltpu.VMEM)
    return pl.pallas_call(
        kernel,
        out_shape=(jax.ShapeDtypeStruct(update_l.shape, F32), jax.ShapeDtypeStruct(pivot_diag.shape, F32)),
        in_specs=[pl.BlockSpec(memory_space=pltpu.SMEM), vmem, vmem, vmem],
        out_specs=(vmem, vmem),
        scratch_shapes=[
            pltpu.VMEM((chunks, width, cols), F32),
            pltpu.VMEM((chunks, width, cols), F32),
            pltpu.VMEM((2, chunks, cols, width), F32),
            pltpu.VMEM((chunks, 2, cols, width), BF16),
            pltpu.VMEM((chunks, 2, cols, width), BF16),
            pltpu.VMEM((rows, cols), F32),
            pltpu.VMEM((4, 2, rows, cols), F32),
            pltpu.VMEM((4, 2, rows, cols), BF16),
            pltpu.VMEM((4, 2, rows, cols), BF16),
            pltpu.VMEM((4, chunks, rows, width), F32),
            pltpu.VMEM((4, chunks, rows // 2, width), F32),
            pltpu.VMEM((4, chunks, rows // 4, width), F32),
            pltpu.VMEM((4, chunks, rows // 4, width), F32),
            pltpu.VMEM((4, chunks, rows // 4, width), F32),
            pltpu.VMEM((chunks, rows, width), F32),
            pltpu.VMEM((8, tile // 8, rows), F32),
            pltpu.VMEM((8, tile // 8, rows), F32),
            pltpu.VMEM((16, tile // 8, rows), F32),
            sem((chunks,)), sem((chunks,)), sem((chunks,)), sem((chunks,)),
            sem, sem, sem((4,)), sem((4,)), sem((4, 2)),
            sem((4, chunks)), sem((4, chunks)), sem((4, chunks)), sem((4, chunks)),
            sem((4, chunks)), sem((4, chunks)), sem((4, chunks)), sem((chunks, 2, 2)),
            sem((8,)), sem((8,)), sem((16,)), sem((16,)),
        ],
        compiler_params=pltpu.CompilerParams(
            collective_id=0, has_side_effects=True, vmem_limit_bytes=62 * 2**20),
        name="selected_inverse",
    )(update_map, root_sigma.reshape(-1, tile, root_sigma.shape[1]), pivot_diag, update_l)


def solution(mesh):
    placed = (P("prow", "pcol"), P(None, None, "prow"), P("prow", "pcol"), P())
    return jax.shard_map(
        local,
        mesh=mesh,
        in_specs=placed,
        out_specs=(P("prow", "pcol"), P(None, None, "prow")),
        check_vma=False,
    )
```

time: 187 us -> 182 us (0.973)
  Pallas kernels: 183 us -> 178 us
    pallas_call x1, Pallas kernels: 183 us -> 178 us  [local(): pl.pallas_call(kernel, out_shape=(jax.ShapeDtypeStruct(update_l.shape, F3...]
where the time goes in v2:
time: 182 us
  Pallas kernels  178 us (98%)
  local copies, waits for them, and re-layouts  3.16 us (2%)
    pallas_call x1, Pallas kernels, local(): pl.pallas_call(kernel, out_shape=(jax.ShapeDtypeStruct(update_l.shape, F3...  178 us

profile of v2, /device:TPU:1, one launch (start us, length us, event | category | flops | bytes accessed | tf_op | source)
XLA Modules:
  0.0 182.2 jit_solution(11580033045938984535)
XLA Ops:
  0.6 178.4 %selected_inverse.1 = (f32[384,768]{1,0:T(8,128)}, f32[128,2,384]{2,1,0:T(2,128)}) custom-call(s32[2,48]{1,0:T(2,128)} %umap.1, f32[12,128,768]{2,1,0:T(8,128)} %bitcast.1, f32[128,2,384]{2,1,0:T(2,128)} %pd.1, f32[384,768]{1,0:T(8,128)} %l_ref.1), custom_call_target="tpu_custom_call" | custom-call | tf_op jit(solution)/shard_map/selected_inverse/pallas_call | solution.py:308
  179.0 0.0 copy-start
  179.0 2.4 %copy.8 = f32[384,768]{1,0:T(8,128)} copy(f32[384,768]{1,0:T(8,128)} %get-tuple-element.4) | data formatting | bytes 2359296
  181.4 0.0 copy-done
  181.4 0.7 copy.9
Async XLA Ops:
  179.0 2.4 %copy-start = (f32[128,2,384]{2,1,0:T(2,128)S(1)}, f32[128,2,384]{2,1,0:T(2,128)}, u32[]{:S(2)}) copy-start(f32[128,2,384]{2,1,0:T(2,128)} %get-tuple-element.5) | copy-start | bytes 1179652

commit v3 on v2

--- a/solution.py
+++ b/solution.py
@@ -16,7 +16,7 @@
 
 
 def kernel(umap, sig, pd, l_ref, c_out, m_out, fs, rc, stf, bhi, blo, lx, lb, ahi, alo, prod, xr, zr, fin, leg, got, dsend, dr, g,
-           zs_s, zs_r, cs_s, cs_r, lx_s, lx_r, l_s, f_s, l_r, x_s, x_r, z_s, z_r, a_s, a_r, b_s, b_r, d_s, d_r, g_s, g_r):
+           zs_s, zs_r, cs_s, cs_r, lx_s, lx_r, l_s, f_s, o_s, l_r, x_s, x_r, z_s, z_r, a_s, a_r, b_s, b_r, d_s, d_r, g_s, g_r):
     me_r, me_c = lax.axis_index("prow"), lax.axis_index("pcol")
     y, xh = me_r // 2, me_r % 2
     half, j = me_c // 8, me_c % 8
@@ -61,7 +61,7 @@
         return copy(src, lb.at[y, k], sems.at[d], l_r.at[y, k], dev((y + d) % 4, xh, zl, xl, core))
 
     def spread_start(src, core, sems):
-        for d in (1, 3, 2):
+        for d in (1, 3):
             spread(src, core, sems, d).start()
 
         @pl.when(k != core)
@@ -73,12 +73,16 @@
             pltpu.make_async_copy(src, lb.at[y, core], l_r.at[y, core]).start()
 
     def spread_end(src, core, sems):
-        for d in (1, 3, 2):
+        for d in (1, 3):
             spread(src, core, sems, d).wait_send()
 
         @pl.when(k != core)
         def _():
             spread(src, core, sems, 0).wait_send()
+
+    def onward(t):
+        yf, yt, kk = (y + 1 + 2 * (t - 1)) % 4, (y + 3 - 2 * (t - 1)) % 4, 2 - t
+        return copy(lb.at[yf, kk], lb.at[yf, kk], o_s.at[t - 1], l_r.at[yf, kk], dev(yt, xh, zl, xl, k))
 
     cross().start()
 
@@ -167,6 +171,10 @@
                     ahi[t, kk] = hi
                     alo[t, kk] = lo
 
+                @pl.when((t == 1) | (t == 2))
+                def _():
+                    onward(t).start()
+
             total = jnp.zeros((rows, width), F32)
             for kk in range(2):
                 total += jnp.dot(ahi[t, kk], bhi[q, kk], preferred_element_type=F32)
@@ -272,6 +280,8 @@
     cross().wait_send()
     spread_end(l_ref, 0, l_s)
     spread_end(lx, 1, f_s)
+    for t in (1, 2):
+        onward(t).wait_send()
     for q in range(chunks):
         far_copy(q).wait_send()
         core_copy(k, q).wait_send()
@@ -330,7 +340,7 @@
             pltpu.VMEM((8, tile // 8, rows), F32),
             pltpu.VMEM((16, tile // 8, rows), F32),
             sem((chunks,)), sem((chunks,)), sem((chunks,)), sem((chunks,)),
-            sem, sem, sem((4,)), sem((4,)), sem((4, 2)),
+            sem, sem, sem((4,)), sem((4,)), sem((2,)), sem((4, 2)),
             sem((4, chunks)), sem((4, chunks)), sem((4, chunks)), sem((4, chunks)),
             sem((4, chunks)), sem((4, chunks)), sem((4, chunks)), sem((chunks, 2, 2)),
             sem((8,)), sem((8,)), sem((16,)), sem((16,)),

time: 182 us -> 154 us (0.85)
  Pallas kernels: 178 us -> 149 us
    pallas_call x1, Pallas kernels: 178 us -> 149 us  [local(): pl.pallas_call(kernel, out_shape=(jax.ShapeDtypeStruct(update_l.shape, F3...]
where the time goes in v3:
time: 154 us; the launch traced here: 152 us
  Pallas kernels  149 us (97%)
  local copies, waits for them, and re-layouts  3.16 us (2%)
    pallas_call x1, Pallas kernels, local(): pl.pallas_call(kernel, out_shape=(jax.ShapeDtypeStruct(update_l.shape, F3...  149 us
    unnamed x4, local copies, waits for them, and re-layouts  3.16 us

profile of v3, /device:TPU:1, one launch (start us, length us, event | category | flops | bytes accessed | tf_op | source)
XLA Modules:
  0.0 152.5 jit_solution(1888200273214171608)
XLA Ops:
  0.6 148.7 %selected_inverse.1 = (f32[384,768]{1,0:T(8,128)}, f32[128,2,384]{2,1,0:T(2,128)}) custom-call(s32[2,48]{1,0:T(2,128)} %umap.1, f32[12,128,768]{2,1,0:T(8,128)} %bitcast.1, f32[128,2,384]{2,1,0:T(2,128)} %pd.1, f32[384,768]{1,0:T(8,128)} %l_ref.1), custom_call_target="tpu_custom_call" | custom-call | tf_op jit(solution)/shard_map/selected_inverse/pallas_call | solution.py:318
  149.3 0.0 copy-start
  149.3 2.4 %copy.8 = f32[384,768]{1,0:T(8,128)} copy(f32[384,768]{1,0:T(8,128)} %get-tuple-element.4) | data formatting | bytes 2359296
  151.7 0.0 copy-done
  151.7 0.7 copy.9
Async XLA Ops:
  149.3 2.4 %copy-start = (f32[128,2,384]{2,1,0:T(2,128)S(1)}, f32[128,2,384]{2,1,0:T(2,128)}, u32[]{:S(2)}) copy-start(f32[128,2,384]{2,1,0:T(2,128)} %get-tuple-element.5) | copy-start | bytes 1179652

commit v4 on v3

--- a/solution.py
+++ b/solution.py
@@ -15,8 +15,8 @@
     return hi, (x - hi.astype(F32)).astype(BF16)
 
 
-def kernel(umap, sig, pd, l_ref, c_out, m_out, fs, rc, stf, bhi, blo, lx, lb, ahi, alo, prod, xr, zr, fin, leg, got, dsend, dr, g,
-           zs_s, zs_r, cs_s, cs_r, lx_s, lx_r, l_s, f_s, o_s, l_r, x_s, x_r, z_s, z_r, a_s, a_r, b_s, b_r, d_s, d_r, g_s, g_r):
+def kernel(umap, sig_in, pd, l_in, c_out, m_out, sig, l_ref, lhi, llo, fs, rc, stf, bhi, blo, lx, lb, ahi, alo, prod, xr, zr, fin, leg, got, dsend, dr, g,
+           in_s, zs_s, zs_r, cs_s, cs_r, lx_s, lx_r, l_s, f_s, o_s, l_r, x_s, x_r, z_s, z_r, a_s, a_r, b_s, b_r, d_s, d_r, g_s, g_r):
     me_r, me_c = lax.axis_index("prow"), lax.axis_index("pcol")
     y, xh = me_r // 2, me_r % 2
     half, j = me_c // 8, me_c % 8
@@ -33,12 +33,15 @@
 
     partner = (me_r, (me_c + 8) % 16)
     other_core = dev(y, xh, zl, xl, 1 - k)
-    x_peer = dev(y, xh, zl, 1 - xl, k)
-    z_peer = dev(y, xh, 1 - zl, xl, k)
 
     def copy(src, dst, ssem, rsem, to):
         return pltpu.make_async_remote_copy(
             src_ref=src, dst_ref=dst, send_sem=ssem, recv_sem=rsem, device_id=to, device_id_type=MESH)
+
+    load_l = pltpu.make_async_copy(l_in, l_ref, in_s.at[0])
+    load_sig = pltpu.make_async_copy(sig_in, sig, in_s.at[1])
+    load_l.start()
+    load_sig.start()
 
     barrier = pltpu.get_barrier_semaphore()
 
@@ -84,18 +87,22 @@
         yf, yt, kk = (y + 1 + 2 * (t - 1)) % 4, (y + 3 - 2 * (t - 1)) % 4, 2 - t
         return copy(lb.at[yf, kk], lb.at[yf, kk], o_s.at[t - 1], l_r.at[yf, kk], dev(yt, xh, zl, xl, k))
 
+    load_l.wait()
     cross().start()
+    spread_start(l_ref, 0, l_s)
 
     def far_copy(q):
         return copy(fs.at[q], rc.at[q], zs_s.at[q], zs_r.at[q], partner)
 
+    load_sig.wait()
     for q in range(chunks):
         for h in range(2):
             row = umap[1 - half, me_r * tiles + 2 * q + h] // 8
             fs[q, h * tile:(h + 1) * tile, :] = sig[row]
         far_copy(q).start()
-
-    spread_start(l_ref, 0, l_s)
+    hi, lo = split(l_ref[...])
+    lhi[...] = hi
+    llo[...] = lo
 
     def core_copy(kk, q):
         return copy(stf.at[kk, q], stf.at[kk, q], cs_s.at[q], cs_r.at[q], other_core)
@@ -129,27 +136,98 @@
         q = (1 - k) * ((1 - last) * (n // 3) + last * (n - 3 * chunks)) + k * (n % chunks)
         return t, q, t + (t // 2) * (1 - 2 * (t % 2))
 
+    def order(q):
+        f = q // (chunks - 1)
+        return f, f * zl + (1 - f) * xl, f * xl + (1 - f) * zl
+
+    def peer(f):
+        return dev(y, xh, zl + f * (1 - 2 * zl), xl + (1 - f) * (1 - 2 * xl), k)
+
     def x_copy(t, q):
-        return copy(prod.at[t, q, pl.ds(2 * part * (1 - xl), 2 * part)], xr.at[t, q], x_s.at[t, q], x_r.at[t, q], x_peer)
+        f, b1, _ = order(q)
+        return copy(prod.at[t, q, pl.ds(2 * part * (1 - b1), 2 * part)], xr.at[t, q], x_s.at[t, q], x_r.at[t, q], peer(f))
 
     def z_copy(t, q):
-        return copy(xr.at[t, q, pl.ds(part * (1 - zl), part)], zr.at[t, q], z_s.at[t, q], z_r.at[t, q], z_peer)
+        f, _, b2 = order(q)
+        return copy(xr.at[t, q, pl.ds(part * (1 - b2), part)], zr.at[t, q], z_s.at[t, q], z_r.at[t, q], peer(1 - f))
+
+    def spot_of(q):
+        _, b1, b2 = order(q)
+        return pl.ds(2 * part * b1 + part * b2, part)
 
     def a_copy(t, q, dy):
         return copy(fin.at[t, q], leg.at[y, q], a_s.at[t, q], a_r.at[y, q], dev((y + dy) % 4, (xh + k) % 2, zl, xl, k))
 
-    spot_b = pl.ds(2 * part * xl + part * zl, part)
-
     def b_copy(ys, q):
-        return copy(leg.at[ys, q], got.at[q, spot_b], b_s.at[ys, q], b_r.at[q, xl, zl], dev(y, xh, ys // 2, ys % 2, (xh + k) % 2))
+        _, b1, b2 = order(q)
+        return copy(leg.at[ys, q], got.at[q, spot_of(q)], b_s.at[ys, q], b_r.at[q, b1, b2], dev(y, xh, ys // 2, ys % 2, (xh + k) % 2))
 
     def b_stays(ys):
         return (ys == 2 * zl + xl) & (xh == 0)
 
     lag_x, lag_z, lag_a = 2, 4, 6
-
-    def step(n, carry):
-        @pl.when(n < steps)
+    gap_1, gap_2 = 2, 4
+    turns = steps + gap_1 + gap_2
+
+    def at_turn(v):
+        after_1 = jnp.where(v >= chunks + gap_1, 1, 0)
+        after_2 = jnp.where(v >= 3 * chunks + gap_1 + gap_2, 1, 0)
+        n = v - gap_1 * after_1 - gap_2 * after_2
+        busy = (v >= 0) & (n < chunks + (2 * chunks) * after_1 + chunks * after_2)
+        return busy, n
+
+    def turn(v, carry):
+        busy, n = at_turn(v - lag_a)
+
+        @pl.when(busy)
+        def _():
+            t, q, dy = where_of(n)
+            ys = (y + 4 - dy) % 4
+
+            @pl.when((t > 0) | (k > 0))
+            def _():
+                copy(leg.at[ys, q], leg.at[ys, q], a_s.at[0, 0], a_r.at[ys, q], other_core).wait_recv()
+
+            @pl.when(b_stays(ys))
+            def _():
+                got[q, spot_of(q)] = leg[ys, q]
+
+            @pl.when(jnp.logical_not(b_stays(ys)))
+            def _():
+                b_copy(ys, q).start()
+
+        busy, n = at_turn(v - lag_z)
+
+        @pl.when(busy)
+        def _():
+            t, q, dy = where_of(n)
+            _, _, b2 = order(q)
+            z_copy(t, q).wait_recv()
+            done = -(xr[t, q, pl.ds(part * b2, part)] + zr[t, q])
+            here = (t == 0) & (k == 0)
+
+            @pl.when(here)
+            def _():
+                leg[y, q] = done
+
+            @pl.when(jnp.logical_not(here))
+            def _():
+                fin[t, q] = done
+                a_copy(t, q, dy).start()
+
+        busy, n = at_turn(v - lag_x)
+
+        @pl.when(busy)
+        def _():
+            t, q, _ = where_of(n)
+            _, b1, _ = order(q)
+            x_copy(t, q).wait_recv()
+            xr[t, q] = xr[t, q] + prod[t, q, pl.ds(2 * part * b1, 2 * part)]
+            z_copy(t, q).start()
+
+        busy, n = at_turn(v)
+
+        @pl.when(busy)
         def _():
             t, q, dy = where_of(n)
             yp = (y + dy) % 4
@@ -167,13 +245,15 @@
             def _():
                 for kk in range(2):
                     copy(lb.at[yp, kk], lb.at[yp, kk], l_s.at[0], l_r.at[yp, kk], other_core).wait_recv()
+
+                @pl.when((t == 1) | (t == 2))
+                def _():
+                    onward(t).start()
+
+                for kk in range(2):
                     hi, lo = split(lb[yp, kk])
                     ahi[t, kk] = hi
                     alo[t, kk] = lo
-
-                @pl.when((t == 1) | (t == 2))
-                def _():
-                    onward(t).start()
 
             total = jnp.zeros((rows, width), F32)
             for kk in range(2):
@@ -182,66 +262,26 @@
                 total += jnp.dot(alo[t, kk], bhi[q, kk], preferred_element_type=F32)
             prod[t, q] = total
             x_copy(t, q).start()
-
-        @pl.when((n >= lag_x) & (n < steps + lag_x))
-        def _():
-            t, q, _ = where_of(n - lag_x)
-            x_copy(t, q).wait_recv()
-            xr[t, q] = xr[t, q] + prod[t, q, pl.ds(2 * part * xl, 2 * part)]
-            z_copy(t, q).start()
-
-        @pl.when((n >= lag_z) & (n < steps + lag_z))
-        def _():
-            t, q, dy = where_of(n - lag_z)
-            z_copy(t, q).wait_recv()
-            done = -(xr[t, q, pl.ds(part * zl, part)] + zr[t, q])
-            here = (t == 0) & (k == 0)
-
-            @pl.when(here)
-            def _():
-                leg[y, q] = done
-
-            @pl.when(jnp.logical_not(here))
-            def _():
-                fin[t, q] = done
-                a_copy(t, q, dy).start()
-
-        @pl.when(n >= lag_a)
-        def _():
-            t, q, dy = where_of(n - lag_a)
-            ys = (y + 4 - dy) % 4
-
-            @pl.when((t > 0) | (k > 0))
-            def _():
-                copy(leg.at[ys, q], leg.at[ys, q], a_s.at[0, 0], a_r.at[ys, q], other_core).wait_recv()
-
-            @pl.when(b_stays(ys))
-            def _():
-                got[q, spot_b] = leg[ys, q]
-
-            @pl.when(jnp.logical_not(b_stays(ys)))
-            def _():
-                b_copy(ys, q).start()
         return carry
 
-    lax.fori_loop(0, steps + lag_a, step, 0)
+    lax.fori_loop(0, turns + lag_a, turn, 0)
 
     diag = [jnp.zeros((tile, tile), F32) for _ in range(rows // tile)]
     for q in range(chunks):
-        for xs in range(2):
-            for zs in range(2):
-                here = (zs == zl) & (xs == xl) & (xh == 0)
-
-                @pl.when(jnp.logical_not(here))
+        _, b1, b2 = order(q)
+        for u in range(2):
+            for v in range(2):
+                @pl.when(jnp.logical_not((u == b1) & (v == b2) & (xh == 0)))
                 def _():
-                    spot = got.at[q, pl.ds(2 * part * xs + part * zs, part)]
-                    copy(spot, spot, b_s.at[0, 0], b_r.at[q, xs, zs], other_core).wait_recv()
+                    spot = got.at[q, pl.ds(2 * part * u + part * v, part)]
+                    copy(spot, spot, b_s.at[0, 0], b_r.at[q, u, v], other_core).wait_recv()
         cols = slice(q * width, (q + 1) * width)
         c_out[:, cols] = got[q]
         for t in range(len(diag)):
             span = slice(t * tile, (t + 1) * tile)
-            diag[t] += lax.dot_general(got[q, span], l_ref[span, cols], NT, precision=lax.Precision.HIGHEST,
-                                       preferred_element_type=F32)
+            hi, lo = split(got[q, span])
+            for left, right in ((hi, lhi), (hi, llo), (lo, lhi)):
+                diag[t] += lax.dot_general(left, right[span, cols], NT, preferred_element_type=F32)
     for t in range(len(diag)):
         dsend[:, :, t * tile:(t + 1) * tile] = diag[t].reshape(8, tile // 8, tile)
 
@@ -315,12 +355,17 @@
     width = cols // chunks
     sem = pltpu.SemaphoreType.DMA
     vmem = pl.BlockSpec(memory_space=pltpu.VMEM)
+    anywhere = pl.BlockSpec(memory_space=pl.ANY)
     return pl.pallas_call(
         kernel,
         out_shape=(jax.ShapeDtypeStruct(update_l.shape, F32), jax.ShapeDtypeStruct(pivot_diag.shape, F32)),
-        in_specs=[pl.BlockSpec(memory_space=pltpu.SMEM), vmem, vmem, vmem],
+        in_specs=[pl.BlockSpec(memory_space=pltpu.SMEM), anywhere, vmem, anywhere],
         out_specs=(vmem, vmem),
         scratch_shapes=[
+            pltpu.VMEM((root_sigma.shape[0] // tile, tile, root_sigma.shape[1]), F32),
+            pltpu.VMEM((rows, cols), F32),
+            pltpu.VMEM((rows, cols), BF16),
+            pltpu.VMEM((rows, cols), BF16),
             pltpu.VMEM((chunks, width, cols), F32),
             pltpu.VMEM((chunks, width, cols), F32),
             pltpu.VMEM((2, chunks, cols, width), F32),
@@ -339,6 +384,7 @@
             pltpu.VMEM((8, tile // 8, rows), F32),
             pltpu.VMEM((8, tile // 8, rows), F32),
             pltpu.VMEM((16, tile // 8, rows), F32),
+            sem((2,)),
             sem((chunks,)), sem((chunks,)), sem((chunks,)), sem((chunks,)),
             sem, sem, sem((4,)), sem((4,)), sem((2,)), sem((4, 2)),
             sem((4, chunks)), sem((4, chunks)), sem((4, chunks)), sem((4, chunks)),

time: 154 us -> 169 us (1.097)
  Pallas kernels: 149 us -> 165 us
    pallas_call x1, Pallas kernels: 149 us -> 165 us  [local(): pl.pallas_call(kernel, out_shape=(jax.ShapeDtypeStruct(update_l.shape, F3...]
where the time goes in v4:
time: 169 us
  Pallas kernels  165 us (98%)
  local copies, waits for them, and re-layouts  3.16 us (2%)
    pallas_call x1, Pallas kernels, local(): pl.pallas_call(kernel, out_shape=(jax.ShapeDtypeStruct(update_l.shape, F3...  165 us

profile of v4, /device:TPU:1, one launch (start us, length us, event | category | flops | bytes accessed | tf_op | source)
XLA Modules:
  0.0 168.7 jit_solution(17024219513269062732)
XLA Ops:
  0.6 164.9 %selected_inverse.1 = (f32[384,768]{1,0:T(8,128)}, f32[128,2,384]{2,1,0:T(2,128)}) custom-call(s32[2,48]{1,0:T(2,128)} %umap.1, f32[12,128,768]{2,1,0:T(8,128)} %bitcast.1, f32[128,2,384]{2,1,0:T(2,128)} %pd.1, f32[384,768]{1,0:T(8,128)} %l_in.1), custom_call_target="tpu_custom_call" | custom-call | tf_op jit(solution)/shard_map/selected_inverse/pallas_call | solution.py:359
  165.5 0.0 copy-start
  165.5 2.4 %copy.8 = f32[384,768]{1,0:T(8,128)} copy(f32[384,768]{1,0:T(8,128)} %get-tuple-element.4) | data formatting | bytes 2359296
  167.9 0.0 copy-done
  167.9 0.7 copy.9
Async XLA Ops:
  165.5 2.4 %copy-start = (f32[128,2,384]{2,1,0:T(2,128)S(1)}, f32[128,2,384]{2,1,0:T(2,128)}, u32[]{:S(2)}) copy-start(f32[128,2,384]{2,1,0:T(2,128)} %get-tuple-element.5) | copy-start | bytes 1179652

commit v5 on v4

--- a/solution.py
+++ b/solution.py
@@ -50,12 +50,12 @@
 
     for d in range(1, 16):
         greet((me_r, (me_c + d) % 16))
-    for d in range(4):
-        greet(dev((y + d) % 4, 1 - xh, zl, xl, k))
-        if d > 0:
-            for kk in range(2):
-                greet(dev((y + d) % 4, xh, zl, xl, kk))
-    pl.semaphore_wait(barrier, 25)
+    for d in range(1, 4):
+        for kk in range(2):
+            greet(dev((y + d) % 4, xh, zl, xl, kk))
+    for d in range(8):
+        greet((2 * y + 1 - xh, half * 8 + d))
+    pl.semaphore_wait(barrier, 29)
 
     def cross():
         return copy(l_ref, lx, lx_s, lx_r, dev(y, 1 - xh, zl, xl, k))
@@ -156,75 +156,22 @@
         return pl.ds(2 * part * b1 + part * b2, part)
 
     def a_copy(t, q, dy):
-        return copy(fin.at[t, q], leg.at[y, q], a_s.at[t, q], a_r.at[y, q], dev((y + dy) % 4, (xh + k) % 2, zl, xl, k))
+        return copy(fin.at[t, q], leg.at[y, q], a_s.at[t, q], a_r.at[y, q], dev((y + dy) % 4, xh, zl, xl, k))
 
     def b_copy(ys, q):
         _, b1, b2 = order(q)
-        return copy(leg.at[ys, q], got.at[q, spot_of(q)], b_s.at[ys, q], b_r.at[q, b1, b2], dev(y, xh, ys // 2, ys % 2, (xh + k) % 2))
+        to = dev(y, (xh + k) % 2, ys // 2, ys % 2, xh)
+        return copy(leg.at[ys, q], got.at[q, spot_of(q)], b_s.at[ys, q], b_r.at[q, b1, b2], to)
 
     def b_stays(ys):
-        return (ys == 2 * zl + xl) & (xh == 0)
-
-    lag_x, lag_z, lag_a = 2, 4, 6
-    gap_1, gap_2 = 2, 4
-    turns = steps + gap_1 + gap_2
+        return (ys == 2 * zl + xl) & (xh == 0) & (k == 0)
+
+    lag_x, lag_z, lag_a = 2, 4, 8
 
     def at_turn(v):
-        after_1 = jnp.where(v >= chunks + gap_1, 1, 0)
-        after_2 = jnp.where(v >= 3 * chunks + gap_1 + gap_2, 1, 0)
-        n = v - gap_1 * after_1 - gap_2 * after_2
-        busy = (v >= 0) & (n < chunks + (2 * chunks) * after_1 + chunks * after_2)
-        return busy, n
+        return (v >= 0) & (v < steps), v
 
     def turn(v, carry):
-        busy, n = at_turn(v - lag_a)
-
-        @pl.when(busy)
-        def _():
-            t, q, dy = where_of(n)
-            ys = (y + 4 - dy) % 4
-
-            @pl.when((t > 0) | (k > 0))
-            def _():
-                copy(leg.at[ys, q], leg.at[ys, q], a_s.at[0, 0], a_r.at[ys, q], other_core).wait_recv()
-
-            @pl.when(b_stays(ys))
-            def _():
-                got[q, spot_of(q)] = leg[ys, q]
-
-            @pl.when(jnp.logical_not(b_stays(ys)))
-            def _():
-                b_copy(ys, q).start()
-
-        busy, n = at_turn(v - lag_z)
-
-        @pl.when(busy)
-        def _():
-            t, q, dy = where_of(n)
-            _, _, b2 = order(q)
-            z_copy(t, q).wait_recv()
-            done = -(xr[t, q, pl.ds(part * b2, part)] + zr[t, q])
-            here = (t == 0) & (k == 0)
-
-            @pl.when(here)
-            def _():
-                leg[y, q] = done
-
-            @pl.when(jnp.logical_not(here))
-            def _():
-                fin[t, q] = done
-                a_copy(t, q, dy).start()
-
-        busy, n = at_turn(v - lag_x)
-
-        @pl.when(busy)
-        def _():
-            t, q, _ = where_of(n)
-            _, b1, _ = order(q)
-            x_copy(t, q).wait_recv()
-            xr[t, q] = xr[t, q] + prod[t, q, pl.ds(2 * part * b1, 2 * part)]
-            z_copy(t, q).start()
-
         busy, n = at_turn(v)
 
         @pl.when(busy)
@@ -262,16 +209,63 @@
                 total += jnp.dot(alo[t, kk], bhi[q, kk], preferred_element_type=F32)
             prod[t, q] = total
             x_copy(t, q).start()
+
+        busy, n = at_turn(v - lag_x)
+
+        @pl.when(busy)
+        def _():
+            t, q, _ = where_of(n)
+            _, b1, _ = order(q)
+            x_copy(t, q).wait_recv()
+            xr[t, q] = xr[t, q] + prod[t, q, pl.ds(2 * part * b1, 2 * part)]
+            z_copy(t, q).start()
+
+        busy, n = at_turn(v - lag_z)
+
+        @pl.when(busy)
+        def _():
+            t, q, dy = where_of(n)
+            _, _, b2 = order(q)
+            z_copy(t, q).wait_recv()
+            done = -(xr[t, q, pl.ds(part * b2, part)] + zr[t, q])
+
+            @pl.when(t == 0)
+            def _():
+                leg[y, q] = done
+
+            @pl.when(t > 0)
+            def _():
+                fin[t, q] = done
+                a_copy(t, q, dy).start()
+
+        busy, n = at_turn(v - lag_a)
+
+        @pl.when(busy)
+        def _():
+            t, q, dy = where_of(n)
+            ys = (y + 4 - dy) % 4
+
+            @pl.when(t > 0)
+            def _():
+                copy(leg.at[ys, q], leg.at[ys, q], a_s.at[0, 0], a_r.at[ys, q], other_core).wait_recv()
+
+            @pl.when(b_stays(ys))
+            def _():
+                got[q, spot_of(q)] = leg[ys, q]
+
+            @pl.when(jnp.logical_not(b_stays(ys)))
+            def _():
+                b_copy(ys, q).start()
         return carry
 
-    lax.fori_loop(0, turns + lag_a, turn, 0)
+    lax.fori_loop(0, steps + lag_a, turn, 0)
 
     diag = [jnp.zeros((tile, tile), F32) for _ in range(rows // tile)]
     for q in range(chunks):
         _, b1, b2 = order(q)
         for u in range(2):
             for v in range(2):
-                @pl.when(jnp.logical_not((u == b1) & (v == b2) & (xh == 0)))
+                @pl.when(jnp.logical_not((u == b1) & (v == b2) & (xh == 0) & (k == 0)))
                 def _():
                     spot = got.at[q, pl.ds(2 * part * u + part * v, part)]
                     copy(spot, spot, b_s.at[0, 0], b_r.at[q, u, v], other_core).wait_recv()
@@ -332,7 +326,7 @@
         x_copy(t, q).wait_send()
         z_copy(t, q).wait_send()
 
-        @pl.when((t > 0) | (k > 0))
+        @pl.when(t > 0)
         def _():
             a_copy(t, q, dy).wait_send()
 

time: 169 us -> 139 us (0.82)
  Pallas kernels: 165 us -> 135 us
    pallas_call x1, Pallas kernels: 165 us -> 135 us  [local(): pl.pallas_call(kernel, out_shape=(jax.ShapeDtypeStruct(update_l.shape, F3...]
where the time goes in v5:
time: 139 us
  Pallas kernels  135 us (97%)
  local copies, waits for them, and re-layouts  3.16 us (2%)
    pallas_call x1, Pallas kernels, local(): pl.pallas_call(kernel, out_shape=(jax.ShapeDtypeStruct(update_l.shape, F3...  135 us
    unnamed x4, local copies, waits for them, and re-layouts  3.16 us

profile of v5, /device:TPU:1, one launch (start us, length us, event | category | flops | bytes accessed | tf_op | source)
XLA Modules:
  0.0 138.9 jit_solution(10193823957057272952)
XLA Ops:
  0.6 135.1 %selected_inverse.1 = (f32[384,768]{1,0:T(8,128)}, f32[128,2,384]{2,1,0:T(2,128)}) custom-call(s32[2,48]{1,0:T(2,128)} %umap.1, f32[12,128,768]{2,1,0:T(8,128)} %bitcast.1, f32[128,2,384]{2,1,0:T(2,128)} %pd.1, f32[384,768]{1,0:T(8,128)} %l_in.1), custom_call_target="tpu_custom_call" | custom-call | tf_op jit(solution)/shard_map/selected_inverse/pallas_call | solution.py:353
  135.8 0.0 copy-start
  135.8 2.4 %copy.8 = f32[384,768]{1,0:T(8,128)} copy(f32[384,768]{1,0:T(8,128)} %get-tuple-element.4) | data formatting | bytes 2359296
  138.2 0.0 copy-done
  138.2 0.7 copy.9
Async XLA Ops:
  135.8 2.4 %copy-start = (f32[128,2,384]{2,1,0:T(2,128)S(1)}, f32[128,2,384]{2,1,0:T(2,128)}, u32[]{:S(2)}) copy-start(f32[128,2,384]{2,1,0:T(2,128)} %get-tuple-element.5) | copy-start | bytes 1179652

commit v6 on v5

--- a/solution.py
+++ b/solution.py
@@ -15,8 +15,8 @@
     return hi, (x - hi.astype(F32)).astype(BF16)
 
 
-def kernel(umap, sig_in, pd, l_in, c_out, m_out, sig, l_ref, lhi, llo, fs, rc, stf, bhi, blo, lx, lb, ahi, alo, prod, xr, zr, fin, leg, got, dsend, dr, g,
-           in_s, zs_s, zs_r, cs_s, cs_r, lx_s, lx_r, l_s, f_s, o_s, l_r, x_s, x_r, z_s, z_r, a_s, a_r, b_s, b_r, d_s, d_r, g_s, g_r):
+def kernel(umap, sig_in, l_in, c_out, g_out, sig, l_ref, lhi, llo, fs, rc, stf, bhi, blo, lx, lb, ahi, alo, prod, xr, zr, fin, leg, got, dsend, dr, g,
+           in_s, out_s, zs_s, zs_r, cs_s, cs_r, lx_s, lx_r, l_s, f_s, o_s, l_r, x_s, x_r, z_s, z_r, a_s, a_r, b_s, b_r, d_s, d_r, g_s, g_r):
     me_r, me_c = lax.axis_index("prow"), lax.axis_index("pcol")
     y, xh = me_r // 2, me_r % 2
     half, j = me_c // 8, me_c % 8
@@ -88,6 +88,9 @@
         return copy(lb.at[yf, kk], lb.at[yf, kk], o_s.at[t - 1], l_r.at[yf, kk], dev(yt, xh, zl, xl, k))
 
     load_l.wait()
+    def arrived(yf, kk):
+        copy(lb.at[yf, kk], lb.at[yf, kk], l_s.at[0], l_r.at[yf, kk], other_core).wait_recv()
+
     cross().start()
     spread_start(l_ref, 0, l_s)
 
@@ -136,46 +139,88 @@
         q = (1 - k) * ((1 - last) * (n // 3) + last * (n - 3 * chunks)) + k * (n % chunks)
         return t, q, t + (t // 2) * (1 - 2 * (t % 2))
 
-    def order(q):
-        f = q // (chunks - 1)
+    def order(t, q):
+        f = (q // (chunks - 1)) * (t // 2)
         return f, f * zl + (1 - f) * xl, f * xl + (1 - f) * zl
 
     def peer(f):
         return dev(y, xh, zl + f * (1 - 2 * zl), xl + (1 - f) * (1 - 2 * xl), k)
 
     def x_copy(t, q):
-        f, b1, _ = order(q)
+        f, b1, _ = order(t, q)
         return copy(prod.at[t, q, pl.ds(2 * part * (1 - b1), 2 * part)], xr.at[t, q], x_s.at[t, q], x_r.at[t, q], peer(f))
 
     def z_copy(t, q):
-        f, _, b2 = order(q)
+        f, _, b2 = order(t, q)
         return copy(xr.at[t, q, pl.ds(part * (1 - b2), part)], zr.at[t, q], z_s.at[t, q], z_r.at[t, q], peer(1 - f))
 
-    def spot_of(q):
-        _, b1, b2 = order(q)
+    def spot_of(t, q):
+        _, b1, b2 = order(t, q)
         return pl.ds(2 * part * b1 + part * b2, part)
 
     def a_copy(t, q, dy):
         return copy(fin.at[t, q], leg.at[y, q], a_s.at[t, q], a_r.at[y, q], dev((y + dy) % 4, xh, zl, xl, k))
 
+    def t_of(ys):
+        dy = (y + 4 - ys) % 4
+        return dy + (dy // 2) * (1 - 2 * (dy % 2))
+
     def b_copy(ys, q):
-        _, b1, b2 = order(q)
+        t = t_of(ys)
+        _, b1, b2 = order(t, q)
         to = dev(y, (xh + k) % 2, ys // 2, ys % 2, xh)
-        return copy(leg.at[ys, q], got.at[q, spot_of(q)], b_s.at[ys, q], b_r.at[q, b1, b2], to)
+        return copy(leg.at[ys, q], got.at[q, spot_of(t, q)], b_s.at[ys, q], b_r.at[q, b1, b2], to)
 
     def b_stays(ys):
         return (ys == 2 * zl + xl) & (xh == 0) & (k == 0)
 
     lag_x, lag_z, lag_a = 2, 4, 8
 
-    def at_turn(v):
-        return (v >= 0) & (v < steps), v
+    def x_stage(n, carry):
+        t, q, _ = where_of(n)
+        _, b1, _ = order(t, q)
+        x_copy(t, q).wait_recv()
+        xr[t, q] = xr[t, q] + prod[t, q, pl.ds(2 * part * b1, 2 * part)]
+        z_copy(t, q).start()
+        return carry
+
+    def z_stage(n, carry):
+        t, q, dy = where_of(n)
+        _, _, b2 = order(t, q)
+        z_copy(t, q).wait_recv()
+        done = -(xr[t, q, pl.ds(part * b2, part)] + zr[t, q])
+
+        @pl.when(t == 0)
+        def _():
+            leg[y, q] = done
+
+        @pl.when(t > 0)
+        def _():
+            fin[t, q] = done
+            a_copy(t, q, dy).start()
+        return carry
+
+    def a_stage(n, carry):
+        t, q, dy = where_of(n)
+        ys = (y + 4 - dy) % 4
+
+        @pl.when(t > 0)
+        def _():
+            copy(leg.at[ys, q], leg.at[ys, q], a_s.at[0, 0], a_r.at[ys, q], other_core).wait_recv()
+
+        @pl.when(b_stays(ys))
+        def _():
+            got[q, spot_of(t_of(ys), q)] = leg[ys, q]
+
+        @pl.when(jnp.logical_not(b_stays(ys)))
+        def _():
+            b_copy(ys, q).start()
+        return carry
 
     def turn(v, carry):
-        busy, n = at_turn(v)
-
-        @pl.when(busy)
-        def _():
+        @pl.when(v < steps)
+        def _():
+            n = v
             t, q, dy = where_of(n)
             yp = (y + dy) % 4
 
@@ -190,12 +235,17 @@
 
             @pl.when(q == 0)
             def _():
-                for kk in range(2):
-                    copy(lb.at[yp, kk], lb.at[yp, kk], l_s.at[0], l_r.at[yp, kk], other_core).wait_recv()
-
-                @pl.when((t == 1) | (t == 2))
+                arrived(yp, 1)
+
+                @pl.when(t != 2)
                 def _():
-                    onward(t).start()
+                    arrived(yp, 0)
+
+                @pl.when(t == 1)
+                def _():
+                    onward(1).start()
+                    arrived((y + 3) % 4, 0)
+                    onward(2).start()
 
                 for kk in range(2):
                     hi, lo = split(lb[yp, kk])
@@ -210,59 +260,20 @@
             prod[t, q] = total
             x_copy(t, q).start()
 
-        busy, n = at_turn(v - lag_x)
-
-        @pl.when(busy)
-        def _():
-            t, q, _ = where_of(n)
-            _, b1, _ = order(q)
-            x_copy(t, q).wait_recv()
-            xr[t, q] = xr[t, q] + prod[t, q, pl.ds(2 * part * b1, 2 * part)]
-            z_copy(t, q).start()
-
-        busy, n = at_turn(v - lag_z)
-
-        @pl.when(busy)
-        def _():
-            t, q, dy = where_of(n)
-            _, _, b2 = order(q)
-            z_copy(t, q).wait_recv()
-            done = -(xr[t, q, pl.ds(part * b2, part)] + zr[t, q])
-
-            @pl.when(t == 0)
+        for stage, lag in ((x_stage, lag_x), (z_stage, lag_z), (a_stage, lag_a)):
+            @pl.when((v >= lag) & (v < steps + lag))
             def _():
-                leg[y, q] = done
-
-            @pl.when(t > 0)
-            def _():
-                fin[t, q] = done
-                a_copy(t, q, dy).start()
-
-        busy, n = at_turn(v - lag_a)
-
-        @pl.when(busy)
-        def _():
-            t, q, dy = where_of(n)
-            ys = (y + 4 - dy) % 4
-
-            @pl.when(t > 0)
-            def _():
-                copy(leg.at[ys, q], leg.at[ys, q], a_s.at[0, 0], a_r.at[ys, q], other_core).wait_recv()
-
-            @pl.when(b_stays(ys))
-            def _():
-                got[q, spot_of(q)] = leg[ys, q]
-
-            @pl.when(jnp.logical_not(b_stays(ys)))
-            def _():
-                b_copy(ys, q).start()
+                stage(v - lag, 0)
         return carry
 
     lax.fori_loop(0, steps + lag_a, turn, 0)
+
+    def write(q):
+        return pltpu.make_async_copy(got.at[q], c_out.at[:, pl.ds(q * width, width)], out_s.at[q])
 
     diag = [jnp.zeros((tile, tile), F32) for _ in range(rows // tile)]
     for q in range(chunks):
-        _, b1, b2 = order(q)
+        _, b1, b2 = order(t_of(2 * zl + xl), q)
         for u in range(2):
             for v in range(2):
                 @pl.when(jnp.logical_not((u == b1) & (v == b2) & (xh == 0) & (k == 0)))
@@ -270,7 +281,7 @@
                     spot = got.at[q, pl.ds(2 * part * u + part * v, part)]
                     copy(spot, spot, b_s.at[0, 0], b_r.at[q, u, v], other_core).wait_recv()
         cols = slice(q * width, (q + 1) * width)
-        c_out[:, cols] = got[q]
+        write(q).start()
         for t in range(len(diag)):
             span = slice(t * tile, (t + 1) * tile)
             hi, lo = split(got[q, span])
@@ -289,28 +300,6 @@
 
     for d in range(1, 8):
         d_copy(d).start()
-    dr[j] = dsend[j]
-    for d in range(1, 8):
-        d_from(d).wait_recv()
-    total = dr[0]
-    for d in range(1, 8):
-        total += dr[d]
-    g[me_c] = total
-
-    def g_copy(d):
-        return copy(g.at[me_c], g.at[me_c], g_s.at[d], g_r.at[me_c], (me_r, (me_c + d) % 16))
-
-    def g_from(d):
-        frm = (me_c + d) % 16
-        return copy(g.at[frm], g.at[frm], g_s.at[d], g_r.at[frm], (me_r, frm))
-
-    for d in range(1, 16):
-        g_copy(d).start()
-    for d in range(1, 16):
-        g_from(d).wait_recv()
-    for h in range(2):
-        m_out[:, h, :] = pd[:, h, :] - g[h * 8:(h + 1) * 8].reshape(tile, -1)
-
     cross().wait_send()
     spread_end(l_ref, 0, l_s)
     spread_end(lx, 1, f_s)
@@ -336,10 +325,53 @@
         return carry
 
     lax.fori_loop(0, steps, sent, 0)
+    for q in range(chunks):
+        write(q).wait()
+    dr[j] = dsend[j]
+    for d in range(1, 8):
+        d_from(d).wait_recv()
+    total = dr[0]
+    for d in range(1, 8):
+        total += dr[d]
+    g[me_c] = total
+
+    def g_copy(d):
+        return copy(g.at[me_c], g.at[me_c], g_s.at[d], g_r.at[me_c], (me_r, (me_c + 2 * d) % 16))
+
+    def g_from(d):
+        frm = (me_c + 2 * d) % 16
+        return copy(g.at[frm], g.at[frm], g_s.at[d], g_r.at[frm], (me_r, frm))
+
+    def h_copy(d):
+        frm = (me_c + 2 * d) % 16
+        return copy(g.at[frm], g.at[frm], g_s.at[8 + d], g_r.at[frm], other_core)
+
+    def h_from(d):
+        frm = (me_c + 1 - 2 * k + 2 * d) % 16
+        return copy(g.at[frm], g.at[frm], g_s.at[8 + d], g_r.at[frm], other_core)
+
+    for d in range(1, 8):
+        g_copy(d).start()
+    h_copy(0).start()
+    for d in range(1, 8):
+        g_from(d).wait_recv()
+        h_copy(d).start()
+    for d in range(8):
+        h_from(d).wait_recv()
+    g_out[...] = g[...].reshape(g_out.shape)
+
     for d in range(1, 8):
         d_copy(d).wait_send()
-    for d in range(1, 16):
+    for d in range(1, 8):
         g_copy(d).wait_send()
+    for d in range(8):
+        h_copy(d).wait_send()
+
+
+def finish(c_ref, g_ref, pd_ref, c_out, m_out):
+    c_out[...] = c_ref[...]
+    for h in range(2):
+        m_out[:, h, :] = pd_ref[:, h, :] - g_ref[h]
 
 
 def local(root_sigma, pivot_diag, update_l, update_map):
@@ -350,11 +382,11 @@
     sem = pltpu.SemaphoreType.DMA
     vmem = pl.BlockSpec(memory_space=pltpu.VMEM)
     anywhere = pl.BlockSpec(memory_space=pl.ANY)
-    return pl.pallas_call(
+    product, diagonal = pl.pallas_call(
         kernel,
-        out_shape=(jax.ShapeDtypeStruct(update_l.shape, F32), jax.ShapeDtypeStruct(pivot_diag.shape, F32)),
-        in_specs=[pl.BlockSpec(memory_space=pltpu.SMEM), anywhere, vmem, anywhere],
-        out_specs=(vmem, vmem),
+        out_shape=(jax.ShapeDtypeStruct(update_l.shape, F32), jax.ShapeDtypeStruct((2, tile, rows), F32)),
+        in_specs=[pl.BlockSpec(memory_space=pltpu.SMEM), anywhere, anywhere],
+        out_specs=(anywhere, vmem),
         scratch_shapes=[
             pltpu.VMEM((root_sigma.shape[0] // tile, tile, root_sigma.shape[1]), F32),
             pltpu.VMEM((rows, cols), F32),
@@ -378,7 +410,7 @@
             pltpu.VMEM((8, tile // 8, rows), F32),
             pltpu.VMEM((8, tile // 8, rows), F32),
             pltpu.VMEM((16, tile // 8, rows), F32),
-            sem((2,)),
+            sem((2,)), sem((chunks,)),
             sem((chunks,)), sem((chunks,)), sem((chunks,)), sem((chunks,)),
             sem, sem, sem((4,)), sem((4,)), sem((2,)), sem((4, 2)),
             sem((4, chunks)), sem((4, chunks)), sem((4, chunks)), sem((4, chunks)),
@@ -388,7 +420,14 @@
         compiler_params=pltpu.CompilerParams(
             collective_id=0, has_side_effects=True, vmem_limit_bytes=62 * 2**20),
         name="selected_inverse",
-    )(update_map, root_sigma.reshape(-1, tile, root_sigma.shape[1]), pivot_diag, update_l)
+    )(update_map, root_sigma.reshape(-1, tile, root_sigma.shape[1]), update_l)
+    return pl.pallas_call(
+        finish,
+        out_shape=(jax.ShapeDtypeStruct(update_l.shape, F32), jax.ShapeDtypeStruct(pivot_diag.shape, F32)),
+        in_specs=[vmem, vmem, vmem],
+        out_specs=(vmem, vmem),
+        name="write_results",
+    )(product, diagonal, pivot_diag)
 
 
 def solution(mesh):

time: 139 us -> 137 us (0.986)
  local copies, waits for them, and re-layouts: 3.16 us -> 0 us
    unnamed x4 -> x0, local copies, waits for them, and re-layouts: 3.16 us -> none
    pallas_call x0 -> x1, Pallas kernels: none -> 2.69 us  [local(): pl.pallas_call(finish, out_shape=(jax.ShapeDtypeStruct(update_l.shape, F3...]
    pallas_call x1, Pallas kernels: 135 us -> 133 us  [local(): pl.pallas_call(kernel, out_shape=(jax.ShapeDtypeStruct(update_l.shape, F3...]
where the time goes in v6:
time: 137 us
  Pallas kernels  136 us (99%)
    pallas_call x1, Pallas kernels, local(): pl.pallas_call(kernel, out_shape=(jax.ShapeDtypeStruct(update_l.shape, F3...  133 us

profile of v6, /device:TPU:1, one launch (start us, length us, event | category | flops | bytes accessed | tf_op | source)
XLA Modules:
  0.0 136.7 jit_solution(7582346838899307078)
XLA Ops:
  0.6 133.4 %selected_inverse.1 = (f32[384,768]{1,0:T(8,128)}, f32[2,128,384]{2,1,0:T(8,128)}) custom-call(s32[2,48]{1,0:T(2,128)} %umap.1, f32[12,128,768]{2,1,0:T(8,128)} %bitcast.1, f32[384,768]{1,0:T(8,128)} %l_in.1), custom_call_target="tpu_custom_call" | custom-call | tf_op jit(solution)/shard_map/selected_inverse/pallas_call | solution.py:385
  134.1 2.7 %write_results.1 = (f32[384,768]{1,0:T(8,128)}, f32[128,2,384]{2,1,0:T(2,128)}) custom-call(f32[384,768]{1,0:T(8,128)} %get-tuple-element.4.c_ref, f32[2,128,384]{2,1,0:T(8,128)} %get-tuple-element.5.g_ref, f32[128,2,384]{2,1,0:T(2,128)} %pd_ref.1), custom_call_target="tpu_custom_call" | custom-call | tf_op jit(solution)/shard_map/write_results/pallas_call | solution.py:424

commit v7 on v6

--- a/solution.py
+++ b/solution.py
@@ -15,7 +15,7 @@
     return hi, (x - hi.astype(F32)).astype(BF16)
 
 
-def kernel(umap, sig_in, l_in, c_out, g_out, sig, l_ref, lhi, llo, fs, rc, stf, bhi, blo, lx, lb, ahi, alo, prod, xr, zr, fin, leg, got, dsend, dr, g,
+def kernel(umap, sig_in, l_in, c_out, g_out, sig, l_ref, lhi, llo, fs, rc, stf, bhi, blo, lx, lb, ahi, alo, prod, xr, zr, fin, leg, got, dsend, dr, summed,
            in_s, out_s, zs_s, zs_r, cs_s, cs_r, lx_s, lx_r, l_s, f_s, o_s, l_r, x_s, x_r, z_s, z_r, a_s, a_r, b_s, b_r, d_s, d_r, g_s, g_r):
     me_r, me_c = lax.axis_index("prow"), lax.axis_index("pcol")
     y, xh = me_r // 2, me_r % 2
@@ -48,14 +48,22 @@
     def greet(to):
         pl.semaphore_signal(barrier, inc=1, device_id=to, device_id_type=MESH)
 
-    for d in range(1, 16):
-        greet((me_r, (me_c + d) % 16))
-    for d in range(1, 4):
+    greet(dev(y, 1 - xh, zl, xl, k))
+    for d in (1, 3):
         for kk in range(2):
             greet(dev((y + d) % 4, xh, zl, xl, kk))
-    for d in range(8):
-        greet((2 * y + 1 - xh, half * 8 + d))
-    pl.semaphore_wait(barrier, 29)
+    greet(dev((y + 2) % 4, xh, zl, xl, k))
+    for d in range(1, 8):
+        greet((me_r, half * 8 + (j + d) % 8))
+    for d in range(4):
+        greet((me_r, (1 - half) * 8 + 2 * d + k))
+
+    @pl.when(k == 1 - xh)
+    def _():
+        for d in range(4):
+            greet((2 * y + 1 - xh, half * 8 + 2 * d + 1))
+
+    pl.semaphore_wait(barrier, 17 + 4 * k)
 
     def cross():
         return copy(l_ref, lx, lx_s, lx_r, dev(y, 1 - xh, zl, xl, k))
@@ -333,32 +341,36 @@
     total = dr[0]
     for d in range(1, 8):
         total += dr[d]
-    g[me_c] = total
+    summed[...] = total
+
+    stay_g = pltpu.make_async_copy(summed, g_out.at[me_c], g_r.at[me_c])
 
     def g_copy(d):
-        return copy(g.at[me_c], g.at[me_c], g_s.at[d], g_r.at[me_c], (me_r, (me_c + 2 * d) % 16))
+        return copy(summed, g_out.at[me_c], g_s.at[d], g_r.at[me_c], (me_r, (me_c + 2 * d) % 16))
 
     def g_from(d):
         frm = (me_c + 2 * d) % 16
-        return copy(g.at[frm], g.at[frm], g_s.at[d], g_r.at[frm], (me_r, frm))
+        return copy(summed, g_out.at[frm], g_s.at[d], g_r.at[frm], (me_r, frm))
 
     def h_copy(d):
         frm = (me_c + 2 * d) % 16
-        return copy(g.at[frm], g.at[frm], g_s.at[8 + d], g_r.at[frm], other_core)
+        src = summed if d == 0 else g_out.at[frm]
+        return copy(src, g_out.at[frm], g_s.at[8 + d], g_r.at[frm], other_core)
 
     def h_from(d):
         frm = (me_c + 1 - 2 * k + 2 * d) % 16
-        return copy(g.at[frm], g.at[frm], g_s.at[8 + d], g_r.at[frm], other_core)
+        return copy(summed, g_out.at[frm], g_s.at[8 + d], g_r.at[frm], other_core)
 
     for d in range(1, 8):
         g_copy(d).start()
     h_copy(0).start()
+    stay_g.start()
     for d in range(1, 8):
         g_from(d).wait_recv()
         h_copy(d).start()
     for d in range(8):
         h_from(d).wait_recv()
-    g_out[...] = g[...].reshape(g_out.shape)
+    stay_g.wait()
 
     for d in range(1, 8):
         d_copy(d).wait_send()
@@ -377,16 +389,16 @@
 def local(root_sigma, pivot_diag, update_l, update_map):
     tile = pivot_diag.shape[0]
     rows, cols = update_l.shape
-    chunks = 3
+    chunks, parts = 3, 2
     width = cols // chunks
     sem = pltpu.SemaphoreType.DMA
     vmem = pl.BlockSpec(memory_space=pltpu.VMEM)
     anywhere = pl.BlockSpec(memory_space=pl.ANY)
     product, diagonal = pl.pallas_call(
         kernel,
-        out_shape=(jax.ShapeDtypeStruct(update_l.shape, F32), jax.ShapeDtypeStruct((2, tile, rows), F32)),
+        out_shape=(jax.ShapeDtypeStruct(update_l.shape, F32), jax.ShapeDtypeStruct((16, tile // 8, rows), F32)),
         in_specs=[pl.BlockSpec(memory_space=pltpu.SMEM), anywhere, anywhere],
-        out_specs=(anywhere, vmem),
+        out_specs=(anywhere, anywhere),
         scratch_shapes=[
             pltpu.VMEM((root_sigma.shape[0] // tile, tile, root_sigma.shape[1]), F32),
             pltpu.VMEM((rows, cols), F32),
@@ -409,7 +421,7 @@
             pltpu.VMEM((chunks, rows, width), F32),
             pltpu.VMEM((8, tile // 8, rows), F32),
             pltpu.VMEM((8, tile // 8, rows), F32),
-            pltpu.VMEM((16, tile // 8, rows), F32),
+            pltpu.VMEM((tile // 8, rows), F32),
             sem((2,)), sem((chunks,)),
             sem((chunks,)), sem((chunks,)), sem((chunks,)), sem((chunks,)),
             sem, sem, sem((4,)), sem((4,)), sem((2,)), sem((4, 2)),
@@ -424,10 +436,18 @@
     return pl.pallas_call(
         finish,
         out_shape=(jax.ShapeDtypeStruct(update_l.shape, F32), jax.ShapeDtypeStruct(pivot_diag.shape, F32)),
-        in_specs=[vmem, vmem, vmem],
-        out_specs=(vmem, vmem),
+        grid=(parts,),
+        in_specs=[
+            pl.BlockSpec((rows // parts, cols), lambda n: (n, 0)),
+            pl.BlockSpec((2, tile // parts, rows), lambda n: (0, n, 0)),
+            pl.BlockSpec((tile // parts, 2, rows), lambda n: (n, 0, 0)),
+        ],
+        out_specs=(
+            pl.BlockSpec((rows // parts, cols), lambda n: (n, 0)),
+            pl.BlockSpec((tile // parts, 2, rows), lambda n: (n, 0, 0)),
+        ),
         name="write_results",
-    )(product, diagonal, pivot_diag)
+    )(product, diagonal.reshape(2, tile, rows), pivot_diag)
 
 
 def solution(mesh):

time: 137 us -> 136 us (level)
  no operation moved by 1% of the time
where the time goes in v7:
time: 136 us
  Pallas kernels  135 us (99%)
    pallas_call x1, Pallas kernels, local(): pl.pallas_call(kernel, out_shape=(jax.ShapeDtypeStruct(update_l.shape, F3...  133 us

profile of v7, /device:TPU:1, one launch (start us, length us, event | category | flops | bytes accessed | tf_op | source)
XLA Modules:
  0.0 135.9 jit_solution(5656201241950607750)
XLA Ops:
  0.6 132.9 %selected_inverse.1 = (f32[384,768]{1,0:T(8,128)}, f32[16,16,384]{2,1,0:T(8,128)}) custom-call(s32[2,48]{1,0:T(2,128)} %umap.1, f32[12,128,768]{2,1,0:T(8,128)} %bitcast.2, f32[384,768]{1,0:T(8,128)} %l_in.1), custom_call_target="tpu_custom_call" | custom-call | tf_op jit(solution)/shard_map/selected_inverse/pallas_call | solution.py:397
  133.5 2.4 %write_results.1 = (f32[384,768]{1,0:T(8,128)}, f32[128,2,384]{2,1,0:T(2,128)}) custom-call(f32[384,768]{1,0:T(8,128)} %get-tuple-element.4.c_ref, f32[2,128,384]{2,1,0:T(8,128)} %bitcast.3, f32[128,2,384]{2,1,0:T(2,128)} %pd_ref.1), custom_call_target="tpu_custom_call" | custom-call | tf_op jit(solution)/shard_map/write_results/pallas_call | solution.py:436

commit v8 on v7

--- a/solution.py
+++ b/solution.py
@@ -186,10 +186,16 @@
 
     def x_stage(n, carry):
         t, q, _ = where_of(n)
-        _, b1, _ = order(t, q)
+        _, b1, b2 = order(t, q)
         x_copy(t, q).wait_recv()
-        xr[t, q] = xr[t, q] + prod[t, q, pl.ds(2 * part * b1, 2 * part)]
+
+        def add(b):
+            at = pl.ds(part * b, part)
+            xr[t, q, at] = xr[t, q, at] + prod[t, q, pl.ds(2 * part * b1 + part * b, part)]
+
+        add(1 - b2)
         z_copy(t, q).start()
+        add(b2)
         return carry
 
     def z_stage(n, carry):
@@ -268,13 +274,13 @@
             prod[t, q] = total
             x_copy(t, q).start()
 
-        for stage, lag in ((x_stage, lag_x), (z_stage, lag_z), (a_stage, lag_a)):
+        for stage, lag in ((x_stage, lag_x), (z_stage, lag_z), (a_stage, lag_a + k)):
             @pl.when((v >= lag) & (v < steps + lag))
-            def _():
+            def _(lag=lag):
                 stage(v - lag, 0)
         return carry
 
-    lax.fori_loop(0, steps + lag_a, turn, 0)
+    lax.fori_loop(0, steps + lag_a + 1, turn, 0)
 
     def write(q):
         return pltpu.make_async_copy(got.at[q], c_out.at[:, pl.ds(q * width, width)], out_s.at[q])

time: 136 us -> 136 us (level)
  no operation moved by 1% of the time
where the time goes in v8:
time: 136 us
  Pallas kernels  135 us (99%)
    pallas_call x1, Pallas kernels, local(): pl.pallas_call(kernel, out_shape=(jax.ShapeDtypeStruct(update_l.shape, F3...  133 us

profile of v8, /device:TPU:1, one launch (start us, length us, event | category | flops | bytes accessed | tf_op | source)
XLA Modules:
  0.0 135.7 jit_solution(9935248246357877683)
XLA Ops:
  0.6 132.6 %selected_inverse.1 = (f32[384,768]{1,0:T(8,128)}, f32[16,16,384]{2,1,0:T(8,128)}) custom-call(s32[2,48]{1,0:T(2,128)} %umap.1, f32[12,128,768]{2,1,0:T(8,128)} %bitcast.2, f32[384,768]{1,0:T(8,128)} %l_in.1), custom_call_target="tpu_custom_call" | custom-call | tf_op jit(solution)/shard_map/selected_inverse/pallas_call | solution.py:403
  133.3 2.4 %write_results.1 = (f32[384,768]{1,0:T(8,128)}, f32[128,2,384]{2,1,0:T(2,128)}) custom-call(f32[384,768]{1,0:T(8,128)} %get-tuple-element.4.c_ref, f32[2,128,384]{2,1,0:T(8,128)} %bitcast.3, f32[128,2,384]{2,1,0:T(2,128)} %pd_ref.1), custom_call_target="tpu_custom_call" | custom-call | tf_op jit(solution)/shard_map/write_results/pallas_call | solution.py:442

commit v9 on v8

--- a/solution.py
+++ b/solution.py
@@ -63,53 +63,54 @@
         for d in range(4):
             greet((2 * y + 1 - xh, half * 8 + 2 * d + 1))
 
-    pl.semaphore_wait(barrier, 17 + 4 * k)
-
-    def cross():
-        return copy(l_ref, lx, lx_s, lx_r, dev(y, 1 - xh, zl, xl, k))
-
-    def spread(src, core, sems, d):
-        return copy(src, lb.at[y, k], sems.at[d], l_r.at[y, k], dev((y + d) % 4, xh, zl, xl, core))
-
-    def spread_start(src, core, sems):
-        for d in (1, 3):
-            spread(src, core, sems, d).start()
-
-        @pl.when(k != core)
-        def _():
-            spread(src, core, sems, 0).start()
-
-        @pl.when(k == core)
-        def _():
-            pltpu.make_async_copy(src, lb.at[y, core], l_r.at[y, core]).start()
-
-    def spread_end(src, core, sems):
-        for d in (1, 3):
-            spread(src, core, sems, d).wait_send()
-
-        @pl.when(k != core)
-        def _():
-            spread(src, core, sems, 0).wait_send()
-
-    def onward(t):
-        yf, yt, kk = (y + 1 + 2 * (t - 1)) % 4, (y + 3 - 2 * (t - 1)) % 4, 2 - t
-        return copy(lb.at[yf, kk], lb.at[yf, kk], o_s.at[t - 1], l_r.at[yf, kk], dev(yt, xh, zl, xl, k))
-
-    load_l.wait()
-    def arrived(yf, kk):
-        copy(lb.at[yf, kk], lb.at[yf, kk], l_s.at[0], l_r.at[yf, kk], other_core).wait_recv()
-
-    cross().start()
-    spread_start(l_ref, 0, l_s)
-
-    def far_copy(q):
-        return copy(fs.at[q], rc.at[q], zs_s.at[q], zs_r.at[q], partner)
-
     load_sig.wait()
     for q in range(chunks):
         for h in range(2):
             row = umap[1 - half, me_r * tiles + 2 * q + h] // 8
             fs[q, h * tile:(h + 1) * tile, :] = sig[row]
+    pl.semaphore_wait(barrier, 17 + 4 * k)
+
+    def cross():
+        return copy(l_ref, lx, lx_s, lx_r, dev(y, 1 - xh, zl, xl, k))
+
+    def spread(src, core, sems, d):
+        return copy(src, lb.at[y, k], sems.at[d], l_r.at[y, k], dev((y + d) % 4, xh, zl, xl, core))
+
+    def spread_start(src, core, sems):
+        for d in (1, 3):
+            spread(src, core, sems, d).start()
+
+        @pl.when(k != core)
+        def _():
+            spread(src, core, sems, 0).start()
+
+        @pl.when(k == core)
+        def _():
+            pltpu.make_async_copy(src, lb.at[y, core], l_r.at[y, core]).start()
+
+    def spread_end(src, core, sems):
+        for d in (1, 3):
+            spread(src, core, sems, d).wait_send()
+
+        @pl.when(k != core)
+        def _():
+            spread(src, core, sems, 0).wait_send()
+
+    def onward(t):
+        yf, yt, kk = (y + 1 + 2 * (t - 1)) % 4, (y + 3 - 2 * (t - 1)) % 4, 2 - t
+        return copy(lb.at[yf, kk], lb.at[yf, kk], o_s.at[t - 1], l_r.at[yf, kk], dev(yt, xh, zl, xl, k))
+
+    load_l.wait()
+    def arrived(yf, kk):
+        copy(lb.at[yf, kk], lb.at[yf, kk], l_s.at[0], l_r.at[yf, kk], other_core).wait_recv()
+
+    cross().start()
+    spread_start(l_ref, 0, l_s)
+
+    def far_copy(q):
+        return copy(fs.at[q], rc.at[q], zs_s.at[q], zs_r.at[q], partner)
+
+    for q in range(chunks):
         far_copy(q).start()
     hi, lo = split(l_ref[...])
     lhi[...] = hi

time: 136 us -> 135 us (level)
  no operation moved by 1% of the time
where the time goes in v9:
time: 135 us
  Pallas kernels  135 us (100%)
    pallas_call x1, Pallas kernels, local(): pl.pallas_call(kernel, out_shape=(jax.ShapeDtypeStruct(update_l.shape, F3...  132 us

profile of v9, /device:TPU:1, one launch (start us, length us, event | category | flops | bytes accessed | tf_op | source)
XLA Modules:
  0.0 135.3 jit_solution(15631814740753749796)
XLA Ops:
  0.6 132.2 %selected_inverse.1 = (f32[384,768]{1,0:T(8,128)}, f32[16,16,384]{2,1,0:T(8,128)}) custom-call(s32[2,48]{1,0:T(2,128)} %umap.1, f32[12,128,768]{2,1,0:T(8,128)} %bitcast.2, f32[384,768]{1,0:T(8,128)} %l_in.1), custom_call_target="tpu_custom_call" | custom-call | tf_op jit(solution)/shard_map/selected_inverse/pallas_call | solution.py:404
  132.9 2.4 %write_results.1 = (f32[384,768]{1,0:T(8,128)}, f32[128,2,384]{2,1,0:T(2,128)}) custom-call(f32[384,768]{1,0:T(8,128)} %get-tuple-element.4.c_ref, f32[2,128,384]{2,1,0:T(8,128)} %bitcast.3, f32[128,2,384]{2,1,0:T(2,128)} %pd_ref.1), custom_call_target="tpu_custom_call" | custom-call | tf_op jit(solution)/shard_map/write_results/pallas_call | solution.py:443
